TPU v7x, 128 devices: a whole 4x4x4 slice. The times are simulated.
128 devices in a mesh: dp: 32 (over x, y, core), fsdp: 4 (over z).
Axes of the slice: x: 4, y: 4, z: 4, core: 2. Of those that a mesh axis runs over, the one named last changes fastest.
Arguments:
- tokens: bfloat16 [65536, 4608], P(('dp', 'fsdp')), as said below
- rmsnorm_gain_vector: bfloat16 [4608], replicated, may hold values from 0.099609375 to 1.8984375
- tied_query_matrix: bfloat16 [4608, 2048], P('fsdp'), may hold values from -0.09375 to 0.09375
- adapter_down_matrix: bfloat16 [4608, 128], P('fsdp'), may hold values from -0.09375 to 0.09375
- adapter_up_matrix: bfloat16 [128, 2048], replicated, may hold values from -0.5 to 0.5
- depth: int32 [4096], P(('dp', 'fsdp')), may hold values from 1 to 3, as said below
- destination: int32 [4096], P(('dp', 'fsdp')), may hold values from 0 to 31, as said below
- cotangent: bfloat16 [32768, 2048], P(('dp', 'fsdp')), may hold values from -6 to 6
Outputs:
- query: bfloat16 [32768, 2048], P(('dp', 'fsdp'))
- grad_tokens: bfloat16 [65536, 4608], P(('dp', 'fsdp'))
- grad_down: float32 [4608, 128], replicated
- grad_up: float32 [128, 2048], replicated
Inputs may be any that keep to these rules, and one draw needn't show every extreme that they name: Blocks that stop before this recursion have depth 1; the others have depth 2 or 3. `destination`: only entries of surviving blocks are read. Each dp index is named by exactly 16 surviving blocks with its own fsdp index, and by at most 1 surviving blocks of any one device; both bounds are reached in every draw. `tokens`: float values of mixed row and feature scales.
All inputs are finite; a program needn't handle non-finite values.
Results may differ from a plain program's by a relative error of at most 0.0053.
Values may be sent and summed in bfloat16 or wider, within the bound.
No kernel may reach another device: no remote copies, remote signals or barrier semaphores. Data moves between devices by JAX's collectives and lax.ppermute only.
A program may use at most 128 MiB of HBM per device.

v0:
```python
import jax
import jax.numpy as jnp
from jax import lax
from jax.sharding import PartitionSpec as P


def arrange(live, target, dp_count, slot_count):
    blocks = live.shape[0]
    order = jnp.arange(blocks, dtype=jnp.int32)
    same = (target[:, None] == target[None, :]) & live[None, :] & (order[None, :] < order[:, None])
    within = jnp.sum(same.astype(jnp.int32), axis=1)
    slot_of = target * slot_count + within
    places = jnp.arange(dp_count * slot_count, dtype=jnp.int32)
    hits = live[None, :] & (slot_of[None, :] == places[:, None])
    source = jnp.sum(jnp.where(hits, order[None, :], 0), axis=1)
    filled = jnp.any(hits, axis=1)
    return (slot_of, source, filled)


def compact(flags, capacity):
    count = flags.shape[0]
    rank = jnp.cumsum(flags.astype(jnp.int32)) - 1
    wanted = jnp.arange(capacity, dtype=jnp.int32)
    places = jnp.arange(count, dtype=jnp.int32)
    match = flags[None, :] & (rank[None, :] == wanted[:, None])
    pick = jnp.sum(jnp.where(match, places[None, :], 0), axis=1)
    return (pick, jnp.clip(rank, 0, capacity - 1))


def project_surviving(
    input_rows,
    incoming_gradient_rows,
    rmsnorm_gain_vector,
    tied_query_matrix,
    adapter_down_matrix,
    adapter_up_matrix,
):
    xfloat = input_rows.astype(jnp.float32)
    inverse = lax.rsqrt(jnp.mean(xfloat * xfloat, axis=-1, keepdims=True) + 1e-06)
    normed = xfloat * inverse
    gain_f = rmsnorm_gain_vector.astype(jnp.float32)
    normalized_blocks = (normed * gain_f).astype(jnp.bfloat16)
    full_weight, full_down = (
        lax.all_gather(tied_query_matrix, "fsdp", axis=0, tiled=True),
        lax.all_gather(adapter_down_matrix, "fsdp", axis=0, tiled=True),
    )
    shared_output = jnp.dot(normalized_blocks, full_weight, preferred_element_type=jnp.float32)
    lowrank_hidden = jnp.dot(
        normalized_blocks, full_down, preferred_element_type=jnp.float32
    ).astype(jnp.bfloat16)
    projected_query_rows = (
        shared_output
        + jnp.dot(lowrank_hidden, adapter_up_matrix, preferred_element_type=jnp.float32)
    ).astype(jnp.bfloat16)
    gradient_lowrank = jnp.einsum(
        "da,va->dv", incoming_gradient_rows, adapter_up_matrix, preferred_element_type=jnp.float32
    ).astype(jnp.bfloat16)
    gradient_normalized = jnp.einsum(
        "rq,dq->rd", incoming_gradient_rows, full_weight, preferred_element_type=jnp.float32
    )
    gradient_normalized = gradient_normalized + jnp.einsum(
        "rk,dk->rd", gradient_lowrank, full_down, preferred_element_type=jnp.float32
    )
    grad_up = jnp.einsum(
        "rk,rq->kq", lowrank_hidden, incoming_gradient_rows, preferred_element_type=jnp.float32
    )
    grad_down = jnp.einsum(
        "rd,rk->dk", normalized_blocks, gradient_lowrank, preferred_element_type=jnp.float32
    )
    dscaled = gradient_normalized * gain_f
    grad_rows = inverse * (dscaled - normed * jnp.mean(dscaled * normed, axis=-1, keepdims=True))
    return (projected_query_rows, grad_rows.astype(jnp.bfloat16), grad_down, grad_up)


def body(
    tokens,
    rmsnorm_gain_vector,
    tied_query_matrix,
    adapter_down_matrix,
    adapter_up_matrix,
    depth,
    destination,
    cotangent,
):
    dp_count = lax.axis_size("dp")
    blocks = depth.shape[0]
    block_rows = tokens.shape[0] // blocks
    width = tokens.shape[1]
    capacity = cotangent.shape[0] // block_rows
    slot_count = max(1, blocks // dp_count)
    live = depth >= 2
    slot_of, source, filled = arrange(live, destination, dp_count, slot_count)
    flag_send = filled.astype(jnp.bfloat16).reshape(dp_count, slot_count)
    zero_b = jnp.zeros((), jnp.bfloat16)
    token_blocks = tokens.reshape(blocks, block_rows, width)
    send_rows = jnp.where(filled[:, None, None], jnp.take(token_blocks, source, axis=0), zero_b)
    send_rows = send_rows.reshape(dp_count, slot_count, block_rows, width)
    got_rows, got_flags = (
        lax.all_to_all(send_rows, "dp", split_axis=0, concat_axis=0, tiled=True),
        lax.all_to_all(flag_send, "dp", split_axis=0, concat_axis=0, tiled=True),
    )
    flags = got_flags.reshape(-1) > 0.5
    pick, rank = compact(flags, capacity)
    input_rows = jnp.take(got_rows.reshape(dp_count * slot_count, block_rows, width), pick, axis=0)
    query, grad_rows, grad_down, grad_up = project_surviving(
        input_rows.reshape(capacity * block_rows, width),
        cotangent,
        rmsnorm_gain_vector,
        tied_query_matrix,
        adapter_down_matrix,
        adapter_up_matrix,
    )
    back = jnp.take(grad_rows.reshape(capacity, block_rows, width), rank, axis=0)
    back = jnp.where(flags[:, None, None], back, zero_b).reshape(
        dp_count, slot_count, block_rows, width
    )
    returned = lax.all_to_all(back, "dp", split_axis=0, concat_axis=0, tiled=True)
    grad_blocks = jnp.take(
        returned.reshape(dp_count * slot_count, block_rows, width), slot_of, axis=0
    )
    grad_tokens = jnp.where(live[:, None, None], grad_blocks, zero_b).reshape(
        tokens.shape[0], width
    )
    grad_down, grad_up = lax.psum((grad_down, grad_up), ("dp", "fsdp"))
    return (query, grad_tokens, grad_down, grad_up)


def solution(mesh):
    in_specs = (
        P(("dp", "fsdp"), None),
        P(),
        P("fsdp", None),
        P("fsdp", None),
        P(),
        P(("dp", "fsdp")),
        P(("dp", "fsdp")),
        P(("dp", "fsdp"), None),
    )
    out_specs = (P(("dp", "fsdp"), None), P(("dp", "fsdp"), None), P(), P())
    return jax.shard_map(body, mesh=mesh, in_specs=in_specs, out_specs=out_specs, check_vma=False)
```

profile of v0, /device:TPU:1, one launch (start us, length us, event | category | flops | bytes accessed | tf_op | source)
XLA Modules:
  0.0 448.2 jit_solution(3391662864419010734)
XLA Ops:
  9.8 8.6 %all-to-all-start = ((bf16[32,1,1]{2,1,0:T(2,128)(2,1)}), bf16[32,1,1]{2,1,0:T(2,128)(2,1)S(1)}, u32[]{:S(2)}, u32[]{:S(2)}) async-start(bf16[32,1,1]{2,1,0:T(2,128)(2,1)} %copy.18), calls=%async_computation | async-start | bytes 32768 | tf_op jit(solution)/shard_map/all_to_all | solution.py:100
  18.5 5.4 %gather_fusion.2 = bf16[32,16,4608]{2,1,0:T(8,128)(2,1)} fusion(bf16[32,16,4608]{2,1,0:T(8,128)(2,1)} %bitcast.43, s32[1024]{0:T(1024)S(1)} %pad_clamp_fusion.3), kind=kCustom, calls=%fused_computation.clone | custom fusion | bytes 9437312 | tf_op jit(solution)/shard_map/jit(_take)/gather | solution.py:96
  23.9 5.1 %fusion.2 = bf16[32,1,16,4608]{3,2,1,0:T(8,128)(2,1)} fusion(bf16[32,16,4608]{2,1,0:T(8,128)(2,1)} %gather_fusion.2, pred[32]{0:T(512)(128)(4,1)S(1)} %compare_and_fusion.1, pred[32]{0:T(512)(128)(4,1)S(1)} %fusion.7), kind=kLoop, calls=%fused_computation.10 | loop fusion | flops 4718592 | bytes 9437248 | tf_op jit(solution)/shard_map/reshape | solution.py:97
  29.0 7.6 %all-to-all-start.1 = ((bf16[32,1,16,4608]{3,2,1,0:T(8,128)(2,1)}), bf16[32,1,16,4608]{3,2,1,0:T(8,128)(2,1)}, u32[]{:S(2)}, u32[]{:S(2)}) async-start(bf16[32,1,16,4608]{3,2,1,0:T(8,128)(2,1)} %fusion.2), calls=%async_computation.1 | async-start | bytes 9437184 | tf_op jit(solution)/shard_map/all_to_all | solution.py:99
  38.3 4.3 fusion.11
  42.6 52.4 %all-to-all-done.1 = bf16[32,1,16,4608]{3,2,1,0:T(8,128)(2,1)} async-done(((bf16[32,1,16,4608]{3,2,1,0:T(8,128)(2,1)}), bf16[32,1,16,4608]{3,2,1,0:T(8,128)(2,1)}, u32[]{:S(2)}, u32[]{:S(2)}) %all-to-all-start.1) | async-done | bytes 4718624 | tf_op jit(solution)/shard_map/all_to_all | solution.py:99
  95.0 3.0 gather_fusion
  98.9 113.5 %all-gather.3.cloned.1.call-done = bf16[4608,2048]{1,0:T(8,128)(2,1)} async-done(((bf16[1152,2048]{1,0:T(8,128)(2,1)}), bf16[4608,2048]{1,0:T(8,128)(2,1)}) %all-gather.3.cloned.1.call-update) | async-done | bytes 18874384 | tf_op jit(solution)/shard_map/all_gather | solution.py:44
  212.4 12.0 %multiply_reduce_fusion = (f32[256]{0:T(256)S(1)}, f32[256,4608]{1,0:T(8,128)}) fusion(f32[256]{0:T(256)S(1)} %rsqrt.12, bf16[16,16,4608]{2,1,0:T(8,128)(2,1)S(1)} %gather_fusion, pred[256]{0:T(512)(128)(4,1)S(1)} %broadcast_in_dim.108, f32[4608]{0:T(1024)S(1)} %convert_element_type.61, f32[256,4608]{1,0:T(8,128)} %fusion.11, ...), kind=kOutput, calls=%fused_computation.12 | convolution fusion | flops 4840095744 | bytes 31740160 | tf_op jit(solution)/shard_map/rq,dq->rd/dot_general | solution.py:58
  224.4 6.4 %multiply_convert_fusion = (bf16[256,4608]{1,0:T(8,128)(2,1)}, bf16[256,4608]{1,0:T(8,128)(2,1)S(1)}) fusion(f32[256,4608]{1,0:T(8,128)} %get-tuple-element.16, f32[256]{0:T(256)S(1)} %broadcast_multiply_fusion, f32[256]{0:T(256)S(1)} %rsqrt.12, bf16[16,16,4608]{2,1,0:T(8,128)(2,1)} %copy-done.1, pred[256]{0:T(512)(128)(4,1)S(1)} %broadcast_in_dim.108, ...), kind=kLoop, calls=%fused_computation.11 | loop fusion | flops 10616832 | bytes 11817216 | tf_op jit(solution)/shard_map/convert_element_type | solution.py:72
  230.8 4.7 %gather_fusion.1 = bf16[32,16,4608]{2,1,0:T(8,128)(2,1)} fusion(bf16[16,16,4608]{2,1,0:T(8,128)(2,1)} %bitcast.42, s32[1024]{0:T(1024)S(1)} %pad_clamp_fusion.1), kind=kCustom, calls=%fused_computation.3 | custom fusion | bytes 9437312 | tf_op jit(solution)/shard_map/jit(_take)/gather | solution.py:113
  235.5 5.1 %fusion.1 = bf16[32,1,16,4608]{3,2,1,0:T(8,128)(2,1)} fusion(bf16[32,16,4608]{2,1,0:T(8,128)(2,1)} %gather_fusion.1, pred[32]{0:T(512)(128)(4,1)S(1)} %compare_and_fusion.2, pred[32]{0:T(512)(128)(4,1)S(1)} %get-tuple-element.13), kind=kLoop, calls=%fused_computation.7 | loop fusion | flops 4718592 | bytes 9437248 | tf_op jit(solution)/shard_map/jit(_where)/select_n | solution.py:114
  240.6 7.6 %all-to-all-start.2 = ((bf16[32,1,16,4608]{3,2,1,0:T(8,128)(2,1)}), bf16[32,1,16,4608]{3,2,1,0:T(8,128)(2,1)}, u32[]{:S(2)}, u32[]{:S(2)}) async-start(bf16[32,1,16,4608]{3,2,1,0:T(8,128)(2,1)} %fusion.1), calls=%async_computation.2 | async-start | bytes 9437184 | tf_op jit(solution)/shard_map/all_to_all | solution.py:117
  248.5 2.0 convolution_convert_fusion.1
  250.5 1.3 fusion.13
  251.8 2.2 fusion.12
  254.1 1.5 fusion.10
  255.5 10.5 %fusion.3 = bf16[256,2048]{1,0:T(8,128)(2,1)} fusion(f32[256,2048]{1,0:T(8,128)S(1)} %fusion.10, bf16[256,4608]{1,0:T(8,128)(2,1)S(1)} %get-tuple-element.12, bf16[4608,2048]{1,0:T(8,128)(2,1)} %all-gather.3.cloned.1.call-done), kind=kOutput, calls=%fused_computation.17 | convolution fusion | flops 4832886784 | bytes 24379392 | tf_op jit(solution)/shard_map/dot_general | solution.py:47
  266.0 44.1 %all-to-all-done.2 = bf16[32,1,16,4608]{3,2,1,0:T(8,128)(2,1)} async-done(((bf16[32,1,16,4608]{3,2,1,0:T(8,128)(2,1)}), bf16[32,1,16,4608]{3,2,1,0:T(8,128)(2,1)}, u32[]{:S(2)}, u32[]{:S(2)}) %all-to-all-start.2) | async-done | bytes 4718624 | tf_op jit(solution)/shard_map/all_to_all | solution.py:117
  310.2 5.4 %gather_fusion.3 = bf16[32,16,4608]{2,1,0:T(8,128)(2,1)} fusion(bf16[32,16,4608]{2,1,0:T(8,128)(2,1)} %bitcast.10, s32[1024]{0:T(1024)S(1)} %pad_clamp_fusion), kind=kCustom, calls=%fused_computation.1.clone | custom fusion | bytes 9437312 | tf_op jit(solution)/shard_map/jit(_take)/gather | solution.py:118
  315.6 5.2 %select_select_fusion = bf16[32,16,4608]{2,1,0:T(8,128)(2,1)} fusion(bf16[32,16,4608]{2,1,0:T(8,128)(2,1)} %gather_fusion.3, pred[32]{0:T(512)(128)(4,1)S(1)} %get-tuple-element.9, pred[32]{0:T(512)(128)(4,1)S(1)} %broadcast_compare_fusion), kind=kLoop, calls=%fused_computation.8 | loop fusion | flops 4718592 | bytes 9437248 | tf_op jit(solution)/shard_map/jit(_where)/select_n | solution.py:121
  320.8 116.6 %all-reduce.3.cloned.1.call-done = (f32[4608,128]{1,0:T(8,128)}, f32[128,2048]{1,0:T(8,128)}) async-done(((f32[4608,128]{1,0:T(8,128)}, f32[128,2048]{1,0:T(8,128)}), (f32[4608,128]{1,0:T(8,128)}, f32[128,2048]{1,0:T(8,128)})) %all-reduce.3.cloned.1.call-update) | async-done | bytes 3407888 | tf_op jit(solution)/shard_map/psum | solution.py:124
  437.4 3.3 copy.22
  440.7 1.0 copy.23
  (51 shorter events, 5.4 us)
Async XLA Ops:
  7.2 29.4 %copy-start = (bf16[256,2048]{1,0:T(8,128)(2,1)S(1)}, bf16[256,2048]{1,0:T(8,128)(2,1)}, u32[]{:S(2)}) copy-start(bf16[256,2048]{1,0:T(8,128)(2,1)} %param.17) | copy-start | bytes 3145732
  7.2 1.5 copy-start.6
  7.2 1.5 copy-start.5
  7.2 31.1 %all-gather.5.cloned.1.call-start = ((), (), s32[]{:S(2)}) async-start(), calls=%async_computation.4 | async-start | bytes 1474560 | tf_op jit(solution)/shard_map/all_gather | solution.py:45
  7.9 204.4 %all-gather.3.cloned.1.call-start = ((), (), s32[]{:S(2)}) async-start(), calls=%async_computation.3 | async-start | bytes 23592960 | tf_op jit(solution)/shard_map/all_gather | solution.py:44
  9.8 19.2 %all-to-all-start = ((bf16[32,1,1]{2,1,0:T(2,128)(2,1)}), bf16[32,1,1]{2,1,0:T(2,128)(2,1)S(1)}, u32[]{:S(2)}, u32[]{:S(2)}) async-start(bf16[32,1,1]{2,1,0:T(2,128)(2,1)} %copy.18), calls=%async_computation | async-start | bytes 32768 | tf_op jit(solution)/shard_map/all_to_all | solution.py:100
  29.0 7.6 %copy-start.4 = (bf16[4608]{0:T(1024)(128)(2,1)S(1)}, bf16[4608]{0:T(1024)(128)(2,1)}, u32[]{:S(2)}) copy-start(bf16[4608]{0:T(1024)(128)(2,1)} %param.11) | copy-start | bytes 27652
  29.0 7.6 %copy-start.2 = (bf16[128,2048]{1,0:T(8,128)(2,1)S(1)}, bf16[128,2048]{1,0:T(8,128)(2,1)}, u32[]{:S(2)}) copy-start(bf16[128,2048]{1,0:T(8,128)(2,1)} %param.14) | copy-start | bytes 1572868
  29.0 66.0 %all-to-all-start.1 = ((bf16[32,1,16,4608]{3,2,1,0:T(8,128)(2,1)}), bf16[32,1,16,4608]{3,2,1,0:T(8,128)(2,1)}, u32[]{:S(2)}, u32[]{:S(2)}) async-start(bf16[32,1,16,4608]{3,2,1,0:T(8,128)(2,1)} %fusion.2), calls=%async_computation.1 | async-start | bytes 9437184 | tf_op jit(solution)/shard_map/all_to_all | solution.py:99
  98.0 126.4 %copy-start.1 = (bf16[16,16,4608]{2,1,0:T(8,128)(2,1)}, bf16[16,16,4608]{2,1,0:T(8,128)(2,1)S(1)}, u32[]{:S(2)}) copy-start(bf16[16,16,4608]{2,1,0:T(8,128)(2,1)S(1)} %gather_fusion) | copy-start | bytes 7077892
  240.6 69.6 %all-to-all-start.2 = ((bf16[32,1,16,4608]{3,2,1,0:T(8,128)(2,1)}), bf16[32,1,16,4608]{3,2,1,0:T(8,128)(2,1)}, u32[]{:S(2)}, u32[]{:S(2)}) async-start(bf16[32,1,16,4608]{3,2,1,0:T(8,128)(2,1)} %fusion.1), calls=%async_computation.2 | async-start | bytes 9437184 | tf_op jit(solution)/shard_map/all_to_all | solution.py:117
  248.2 189.1 %all-reduce.3.cloned.1.call-start = ((), (), s32[]{:S(2)}) async-start(), calls=%async_computation.5 | async-start | bytes 6815744 | tf_op jit(solution)/shard_map/psum | solution.py:124
  437.4 3.3 copy-start.3
Sparse Core Ops, SparseCore 0:
  9.7 26.8 all-gather.4
  38.3 174.0 all-gather.2
  254.7 182.6 all-reduce.2
where the time goes:
time: 449 us; the launch traced here: 448 us
  waiting for transfers between devices  328 us (73%)
  matrix products  34.3 us (8%)
  other arithmetic  24.1 us (5%)
  starting transfers between devices  24 us (5%)
  local copies, waits for them, and re-layouts  23.8 us (5%)
  between operations  14 us (3%)
    psum x1, waiting for transfers between devices, body(): grad_down, grad_up = lax.psum((grad_down, grad_up), ('dp', 'fsdp'))  117 us
    all_gather x1, waiting for transfers between devices, project_surviving(): lax.all_gather(tied_query_matrix, 'fsdp', axis=0, tiled=True)  113 us
    all_to_all x1, waiting for transfers between devices, body(): lax.all_to_all(send_rows, 'dp', split_axis=0, concat_axis=0, tiled=True)  52.4 us
    all_to_all x1, waiting for transfers between devices, body(): lax.all_to_all(back, 'dp', split_axis=0, concat_axis=0, tiled=True)  44.1 us
    dot_general x1, matrix products, project_surviving(): jnp.einsum('rq,dq->rd', incoming_gradient_rows, full_weight, preferred_el...  12 us
    dot_general x1, matrix products, project_surviving(): jnp.dot(normalized_blocks, full_weight, preferred_element_type=jnp.float32)  10.5 us
  transfers between devices with their start and end apart: 6, of which 4 were waited for; matrix products, arithmetic and copies ran while one was open for 11% of the time, Pallas kernels for 0%

commit v1 on v0

v1 whole, which is shorter than its diff:
```python
import jax
import jax.numpy as jnp
from jax import lax
from jax.sharding import Mesh, PartitionSpec as P

DP = ("x", "y", "core")
BF16 = jnp.bfloat16
F32 = jnp.float32


def dot(a, b, dims=((1,), (0,))):
    return lax.dot_general(a, b, (dims, ((), ())), preferred_element_type=F32)


def gather_down(down):
    me = lax.axis_index("fsdp")
    rows = down.shape[0]
    full = jnp.zeros((4 * rows, down.shape[1]), down.dtype)
    for step in range(4):
        part = down
        if step:
            part = lax.ppermute(down, "fsdp", [((i + step) % 4, i) for i in range(4)])
        full = lax.dynamic_update_slice(full, part, (((me + step) % 4) * rows, 0))
    return full


def gather_weight(weight):
    chip = lax.axis_index("x") * 4 + lax.axis_index("y")
    half = weight.shape[1] // 2
    rows = weight.shape[0] // 16
    piece = lax.dynamic_slice(weight, (chip * rows, lax.axis_index("core") * half), (rows, half))
    both = lax.all_gather(piece, ("core", "fsdp", "x", "y"), axis=0, tiled=True)
    return both.reshape(2, both.shape[0] // 2, half)


def reduce_gradients(grads):
    rows, lanes = grads.shape
    parts = lax.all_to_all(grads.astype(BF16), DP, 0, 0, tiled=True)
    mine = jnp.sum(parts.reshape(32, rows // 32, lanes).astype(F32), axis=0)
    mine = lax.psum(mine, "fsdp")
    return lax.all_gather(mine, DP, axis=0, tiled=True)


def body(tokens, gain, weight, down, up, depth, destination, cotangent):
    blocks = depth.shape[0]
    rows, width = tokens.shape
    block_rows = rows // blocks
    features = cotangent.shape[1]
    capacity = cotangent.shape[0] // block_rows
    live = depth >= 2
    dest = jnp.clip(destination, 0, 31)

    hit = live[None, :] & (dest[None, :] == jnp.arange(32, dtype=jnp.int32)[:, None])
    order = jnp.arange(blocks, dtype=jnp.int32)
    source = jnp.sum(jnp.where(hit, order[None, :], 0), axis=1)
    sent = jnp.any(hit, axis=1).astype(jnp.int32)
    flags = lax.all_to_all(sent, DP, 0, 0, tiled=True)
    rank = jnp.sum(jnp.where(order[None, :] < order[:, None], flags[None, :], 0), axis=1)
    seat = jnp.clip(rank, 0, capacity - 1)
    seats = jnp.arange(capacity, dtype=jnp.int32)
    match = (flags[None, :] > 0) & (rank[None, :] == seats[:, None])
    pick = jnp.sum(jnp.where(match, order[None, :], 0), axis=1)

    full_weight = gather_weight(weight)
    full_down = gather_down(down)

    g_send = jnp.take(cotangent.reshape(capacity, block_rows, features), seat, axis=0)
    g_got = lax.all_to_all(g_send, DP, 0, 0, tiled=True)
    g = jnp.where(live[:, None, None], jnp.take(g_got, dest, axis=0), jnp.zeros((), BF16))
    g = g.reshape(rows, features)

    x = tokens.astype(F32)
    inverse = lax.rsqrt(jnp.mean(x * x, axis=-1, keepdims=True) + 1e-06)
    gain_f = gain.astype(F32)
    xn = (x * inverse * gain_f).astype(BF16)
    low = dot(xn, full_down).astype(BF16)
    dlow = dot(g, up, ((1,), (1,))).astype(BF16)
    grad_up = dot(low, g, ((0,), (0,)))
    grad_down = dot(xn, dlow, ((0,), (0,)))
    grads = jnp.concatenate([grad_down, grad_up.reshape(-1, grad_down.shape[1])], axis=0)
    grads = reduce_gradients(grads)
    grad_down, grad_up = grads[:width], grads[width:].reshape(grad_up.shape)

    half = features // 2
    q = jnp.concatenate([dot(xn, full_weight[0]), dot(xn, full_weight[1])], axis=1)
    q = (q + dot(low, up)).astype(BF16).reshape(blocks, block_rows, features)
    q_got = lax.all_to_all(jnp.take(q, source, axis=0), DP, 0, 0, tiled=True)
    query = jnp.take(q_got, pick, axis=0).reshape(capacity * block_rows, features)

    dxn = dot(g[:, :half], full_weight[0], ((1,), (1,))) + dot(g[:, half:], full_weight[1], ((1,), (1,)))
    dxn = dxn + dot(dlow, full_down, ((1,), (1,)))
    dy = dxn * gain_f
    normed = x * inverse
    grad_tokens = inverse * (dy - normed * jnp.mean(dy * normed, axis=-1, keepdims=True))
    grad_tokens = jnp.where(jnp.repeat(live, block_rows)[:, None], grad_tokens, 0.0).astype(BF16)
    return query, grad_tokens, grad_down, grad_up


def solution(mesh):
    fine = Mesh(mesh.devices.reshape(4, 4, 2, 4), ("x", "y", "core", "fsdp"))
    split = P(("x", "y", "core", "fsdp"))
    in_specs = (split, P(), P("fsdp"), P("fsdp"), P(), split, split, split)
    return jax.shard_map(
        body, mesh=fine, in_specs=in_specs, out_specs=(split, split, P(), P()), check_vma=False
    )
```

time: 449 us -> 357 us (0.80)
  waiting for transfers between devices: 328 us -> 189 us
  blocking collectives: 0 us -> 27.8 us
  matrix products: 34.3 us -> 58.4 us
  other arithmetic: 24.1 us -> 19.5 us
    psum x1, waiting for transfers between devices: 117 us -> 35 us  [reduce_gradients(): mine = lax.psum(mine, 'fsdp')]
    all_to_all x3, waiting for transfers between devices: 96.6 us -> 24.6 us  [the longest x1 21.1 us: body(): g_got = lax.all_to_all(g_send, DP, 0, 0, tiled=True)]
    all_to_all x0 -> x1, blocking collectives: none -> 27.8 us  [reduce_gradients(): parts = lax.all_to_all(grads.astype(BF16), DP, 0, 0, tiled=True)]
    dot_general x8 -> x10, matrix products: 34.3 us -> 58.4 us  [dot(): return lax.dot_general(a, b, (dims, ((), ())), preferred_element_type=F32)]
    all_gather x2, waiting for transfers between devices: 113 us -> 130 us  [the longest x1 81.2 us: gather_weight(): both = lax.all_gather(piece, ('core', 'fsdp', 'x', 'y'), axis=0, tiled=True)]
    gather x4, local copies, waits for them, and re-layouts: 18.5 us -> 8.47 us  [the longest x1 3.59 us: body(): q_got = lax.all_to_all(jnp.take(q, source, axis=0), DP, 0, 0, tiled=True)]
    ppermute x0 -> x3, starting transfers between devices: none -> 5.36 us  [gather_down(): part = lax.ppermute(down, 'fsdp', [((i + step) % 4, i) for i in range(4)])]
    reshape x1 -> x0, other arithmetic: 5.11 us -> none  [body(): send_rows = send_rows.reshape(dp_count, slot_count, block_rows, width)]
  transfers between devices with their start and end apart: 6 -> 9, of which waited for: 4 -> 5; matrix products, arithmetic and copies ran while one was open for 11% -> 16% of each run, Pallas kernels for 0% -> 0%
where the time goes in v1:
time: 357 us; the launch traced here: 356 us
  waiting for transfers between devices  189 us (53%)
  matrix products  58.4 us (16%)
  blocking collectives  27.8 us (8%)
  starting transfers between devices  25.7 us (7%)
  local copies, waits for them, and re-layouts  21.6 us (6%)
  other arithmetic  19.5 us (5%)
  between operations  14.2 us (4%)
    all_gather x1, waiting for transfers between devices, gather_weight(): both = lax.all_gather(piece, ('core', 'fsdp', 'x', 'y'), axis=0, tiled=True)  81.2 us
    dot_general x10, matrix products, dot(): return lax.dot_general(a, b, (dims, ((), ())), preferred_element_type=F32)  58.4 us
    all_gather x1, waiting for transfers between devices, reduce_gradients(): return lax.all_gather(mine, DP, axis=0, tiled=True)  48.4 us
    psum x1, waiting for transfers between devices, reduce_gradients(): mine = lax.psum(mine, 'fsdp')  35 us
    all_to_all x1, blocking collectives, reduce_gradients(): parts = lax.all_to_all(grads.astype(BF16), DP, 0, 0, tiled=True)  27.8 us
    all_to_all x1, waiting for transfers between devices, body(): g_got = lax.all_to_all(g_send, DP, 0, 0, tiled=True)  21.1 us
    all_to_all x1, starting transfers between devices, body(): flags = lax.all_to_all(sent, DP, 0, 0, tiled=True)  8.6 us
    all_to_all x1, starting transfers between devices, body(): q_got = lax.all_to_all(jnp.take(q, source, axis=0), DP, 0, 0, tiled=True)  7.17 us
  transfers between devices with their start and end apart: 9, of which 5 were waited for; matrix products, arithmetic and copies ran while one was open for 16% of the time, Pallas kernels for 0%

profile of v1, /device:TPU:1, one launch (start us, length us, event | category | flops | bytes accessed | tf_op | source)
XLA Modules:
  0.0 356.4 jit_solution(17156562937202370914)
XLA Ops:
  7.2 4.7 %collective-permute-start = (bf16[1152,128]{1,0:T(8,128)(2,1)}, bf16[1152,128]{1,0:T(8,128)(2,1)}, u32[]{:S(2)}, u32[]{:S(2)}) collective-permute-start(bf16[1152,128]{1,0:T(8,128)(2,1)} %param.13), channel_id=1, source_target_pairs={{1,0},{2,1},{3,2},{0,3},{5,4},{6,5},{7,6},{4,7},{9,8},{10,9},{11,1... | collective-permute-start | bytes 884744 | tf_op jit(solution)/shard_map/ppermute | solution.py:22
  14.7 8.6 %all-to-all-start = ((s32[32,1,1]{2,1,0:T(1,128)}), s32[32,1,1]{2,1,0:T(1,128)S(1)}, u32[]{:S(2)}, u32[]{:S(2)}) async-start(s32[32,1,1]{2,1,0:T(1,128)} %copy.14), calls=%async_computation | async-start | bytes 32768 | tf_op jit(solution)/shard_map/all_to_all | solution.py:57
  23.4 3.3 fusion.9
  26.7 3.4 all-to-all-done
  33.3 4.3 %all-to-all-start.2 = ((bf16[32,16,2048]{2,1,0:T(8,128)(2,1)}), bf16[32,16,2048]{2,1,0:T(8,128)(2,1)S(1)}, u32[]{:S(2)}, u32[]{:S(2)}) async-start(bf16[32,16,2048]{2,1,0:T(8,128)(2,1)} %broadcast_select_fusion.1), calls=%async_computation.2 | async-start | bytes 4194304 | tf_op jit(solution)/shard_map/all_to_all | solution.py:68
  41.1 3.8 %convolution_convert_fusion.3 = bf16[512,128]{1,0:T(8,128)(2,1)S(1)} fusion(bf16[4608,128]{1,0:T(8,128)(2,1)S(1)} %constant_dynamic-update-slice_fusion, bf16[512,4608]{1,0:T(8,128)(2,1)} %param.10, f32[4608]{0:T(1024)S(1)} %convert_element_type.45, f32[512]{0:T(512)S(1)} %add_rsqrt_fusion), kind=kOutput, calls=%fused_computation.35 | convolution fusion | flops 613482496 | bytes 6049792 | tf_op jit(solution)/shard_map/dot_general | solution.py:12
  44.9 21.1 %all-to-all-done.2 = bf16[32,16,2048]{2,1,0:T(8,128)(2,1)S(1)} async-done(((bf16[32,16,2048]{2,1,0:T(8,128)(2,1)}), bf16[32,16,2048]{2,1,0:T(8,128)(2,1)S(1)}, u32[]{:S(2)}, u32[]{:S(2)}) %all-to-all-start.2) | async-done | bytes 2097184 | tf_op jit(solution)/shard_map/all_to_all | solution.py:68
  71.4 4.1 %convolution_convert_fusion = bf16[4608,128]{1,0:T(8,128)(2,1)S(1)} fusion(bf16[512,128]{1,0:T(8,128)(2,1)S(1)} %convolution_convert_fusion.2, bf16[512,4608]{1,0:T(8,128)(2,1)} %param.10, f32[4608]{0:T(1024)S(1)} %convert_element_type.45, f32[512]{0:T(512)S(1)} %add_rsqrt_fusion), kind=kOutput, calls=%fused_computation.25 | convolution fusion | flops 614006784 | bytes 6049792 | tf_op jit(solution)/shard_map/dot_general | solution.py:12
  75.6 27.8 %all_to_all.25 = bf16[32,208,128]{2,1,0:T(8,128)(2,1)S(1)} all-to-all(bf16[32,208,128]{2,1,0:T(8,128)(2,1)S(1)} %bitcast.34), channel_id=1, replica_groups=mesh['x'=4,'y'=4,'core'=2,'fsdp'=4] {'x','y','core'}, dimensions={0} | all-to-all | bytes 3407872 | tf_op jit(solution)/shard_map/all_to_all | solution.py:38
  104.4 35.0 %all-reduce.2.cloned.1.call-done = f32[208,128]{1,0:T(8,128)} async-done(((f32[208,128]{1,0:T(8,128)}), f32[208,128]{1,0:T(8,128)}) %all-reduce.2.cloned.1.call-update) | async-done | bytes 106512 | tf_op jit(solution)/shard_map/psum | solution.py:40
  141.8 48.4 %all-gather.5.cloned.1.call-done = f32[6656,128]{1,0:T(8,128)} async-done(((f32[208,128]{1,0:T(8,128)}), f32[6656,128]{1,0:T(8,128)}) %all-gather.5.cloned.1.call-update) | async-done | bytes 3407888 | tf_op jit(solution)/shard_map/all_gather | solution.py:41
  192.6 3.2 slice.40
  195.9 81.2 %all-gather.3.cloned.1.call-done = bf16[9216,1024]{1,0:T(8,128)(2,1)} async-done(((bf16[72,1024]{1,0:T(8,128)(2,1)}), bf16[9216,1024]{1,0:T(8,128)(2,1)}) %all-gather.3.cloned.1.call-update) | async-done | bytes 18874384 | tf_op jit(solution)/shard_map/all_gather | solution.py:32
  277.0 9.2 %fusion.12 = f32[512,1024]{1,0:T(8,128)S(1)} fusion(bf16[9216,1024]{1,0:T(8,128)(2,1)} %all-gather.3.cloned.1.call-done, bf16[512,4608]{1,0:T(8,128)(2,1)} %param.10, f32[4608]{0:T(1024)S(1)} %convert_element_type.45, f32[512]{0:T(512)S(1)} %add_rsqrt_fusion), kind=kOutput, calls=%fused_computation.19 | convolution fusion | flops 4841275392 | bytes 16273408 | tf_op jit(solution)/shard_map/dot_general | solution.py:12
  287.5 7.3 %fusion.16 = f32[512,1024]{1,0:T(8,128)S(1)} fusion(bf16[9216,1024]{1,0:T(8,128)(2,1)S(1)} %copy-done.8, bf16[512,4608]{1,0:T(8,128)(2,1)} %param.10, f32[4608]{0:T(1024)S(1)} %convert_element_type.45, f32[512]{0:T(512)S(1)} %add_rsqrt_fusion), kind=kOutput, calls=%fused_computation.23 | convolution fusion | flops 4841275392 | bytes 16275456 | tf_op jit(solution)/shard_map/dot_general | solution.py:12
  294.8 2.0 fusion.18
  296.9 3.6 %gather_fusion.2 = bf16[32,16,2048]{2,1,0:T(8,128)(2,1)} fusion(bf16[32,16,2048]{2,1,0:T(8,128)(2,1)} %bitcast.33, s32[1024]{0:T(1024)S(1)} %pad_clamp_fusion.3), kind=kCustom, calls=%fused_computation.clone | custom fusion | bytes 4194432 | tf_op jit(solution)/shard_map/jit(_take)/gather | solution.py:87
  300.4 3.2 broadcast_select_fusion
  303.6 7.2 %all-to-all-start.1 = ((bf16[32,16,2048]{2,1,0:T(8,128)(2,1)}), bf16[32,16,2048]{2,1,0:T(8,128)(2,1)}, u32[]{:S(2)}, u32[]{:S(2)}) async-start(bf16[32,16,2048]{2,1,0:T(8,128)(2,1)} %broadcast_select_fusion), calls=%async_computation.1 | async-start | bytes 4194304 | tf_op jit(solution)/shard_map/all_to_all | solution.py:87
  310.8 11.4 %fusion.10 = f32[512,4608]{1,0:T(8,128)} fusion(bf16[9216,1024]{1,0:T(8,128)(2,1)} %all-gather.3.cloned.1.call-done, bf16[512,2048]{1,0:T(8,128)(2,1)S(1)} %bitcast.31), kind=kOutput, calls=%fused_computation.17 | convolution fusion | flops 4831838208 | bytes 19922944 | tf_op jit(solution)/shard_map/dot_general | solution.py:12
  322.2 11.3 %fusion.14 = f32[512,4608]{1,0:T(8,128)} fusion(bf16[9216,1024]{1,0:T(8,128)(2,1)} %all-gather.3.cloned.1.call-done, bf16[512,2048]{1,0:T(8,128)(2,1)S(1)} %bitcast.32), kind=kOutput, calls=%fused_computation.21 | convolution fusion | flops 4831838208 | bytes 19922944 | tf_op jit(solution)/shard_map/dot_general | solution.py:12
  333.5 8.1 %fusion.4 = (f32[512]{0:T(512)S(1)}, f32[512,4608]{1,0:T(8,128)S(1)}) fusion(bf16[512,4608]{1,0:T(8,128)(2,1)S(1)} %bitcast.28, f32[512]{0:T(512)S(1)} %add_rsqrt_fusion, f32[4608]{0:T(1024)S(1)} %convert_element_type.45, bf16[512,128]{1,0:T(8,128)(2,1)S(1)} %convolution_convert_fusion.2, bf16[4608,128]{1,0:T(8,128)(2,1)S(1)} %copy-done.3, ...), kind=kOutput, calls=%fused_computation.10 | convolution fusion | flops 620494336 | bytes 34363392 | tf_op jit(solution)/shard_map/dot_general | solution.py:12
  341.6 4.8 %fusion.8 = bf16[512,4608]{1,0:T(8,128)(2,1)} fusion(f32[512,4608]{1,0:T(8,128)S(1)} %get-tuple-element.8, bf16[512,4608]{1,0:T(8,128)(2,1)S(1)} %bitcast.28, f32[512]{0:T(512)S(1)} %broadcast_multiply_fusion, f32[512]{0:T(512)S(1)} %add_rsqrt_fusion, pred[512]{0:T(512)(128)(4,1)S(1)} %broadcast_in_dim.119), kind=kLoop, calls=%fused_computation.14 | loop fusion | flops 16515072 | bytes 18878976 | tf_op jit(solution)/shard_map/convert_element_type | solution.py:95
  346.5 2.2 gather_fusion
  (83 shorter events, 23.0 us)
Async XLA Ops:
  7.2 23.8 %copy-start = (bf16[256,2048]{1,0:T(8,128)(2,1)S(1)}, bf16[256,2048]{1,0:T(8,128)(2,1)}, u32[]{:S(2)}) copy-start(bf16[256,2048]{1,0:T(8,128)(2,1)} %param.17) | copy-start | bytes 3145732
  7.2 19.5 %copy-start.7 = (bf16[4608]{0:T(1024)(128)(2,1)S(1)}, bf16[4608]{0:T(1024)(128)(2,1)}, u32[]{:S(2)}) copy-start(bf16[4608]{0:T(1024)(128)(2,1)} %param.11) | copy-start | bytes 27652
  7.2 30.8 %collective-permute-start = (bf16[1152,128]{1,0:T(8,128)(2,1)}, bf16[1152,128]{1,0:T(8,128)(2,1)}, u32[]{:S(2)}, u32[]{:S(2)}) collective-permute-start(bf16[1152,128]{1,0:T(8,128)(2,1)} %param.13), channel_id=1, source_target_pairs={{1,0},{2,1},{3,2},{0,3},{5,4},{6,5},{7,6},{4,7},{9,8},{10,9},{11,1... | collective-permute-start | bytes 884744 | tf_op jit(solution)/shard_map/ppermute | solution.py:22
  11.8 27.1 %collective-permute-start.1 = (bf16[1152,128]{1,0:T(8,128)(2,1)}, bf16[1152,128]{1,0:T(8,128)(2,1)}, u32[]{:S(2)}, u32[]{:S(2)}) collective-permute-start(bf16[1152,128]{1,0:T(8,128)(2,1)} %param.13), channel_id=1, source_target_pairs={{2,0},{3,1},{0,2},{1,3},{6,4},{7,5},{4,6},{5,7},{10,8},{11,9},{8,1... | collective-permute-start | bytes 884744 | tf_op jit(solution)/shard_map/ppermute | solution.py:22
  11.9 28.1 %collective-permute-start.2 = (bf16[1152,128]{1,0:T(8,128)(2,1)}, bf16[1152,128]{1,0:T(8,128)(2,1)S(1)}, u32[]{:S(2)}, u32[]{:S(2)}) collective-permute-start(bf16[1152,128]{1,0:T(8,128)(2,1)} %param.13), channel_id=1, source_target_pairs={{3,0},{0,1},{1,2},{2,3},{7,4},{4,5},{5,6},{6,7},{11,8},{8,9},{9,10... | collective-permute-start | bytes 884744 | tf_op jit(solution)/shard_map/ppermute | solution.py:22
  14.7 15.5 %all-to-all-start = ((s32[32,1,1]{2,1,0:T(1,128)}), s32[32,1,1]{2,1,0:T(1,128)S(1)}, u32[]{:S(2)}, u32[]{:S(2)}) async-start(s32[32,1,1]{2,1,0:T(1,128)} %copy.14), calls=%async_computation | async-start | bytes 32768 | tf_op jit(solution)/shard_map/all_to_all | solution.py:57
  31.7 6.2 %copy-start.6 = (bf16[1152,128]{1,0:T(8,128)(2,1)S(1)}, bf16[1152,128]{1,0:T(8,128)(2,1)}, u32[]{:S(2)}) copy-start(bf16[1152,128]{1,0:T(8,128)(2,1)} %param.13) | copy-start | bytes 884740
  31.7 6.2 %copy-start.9 = (s32[32]{0:T(128)S(1)}, s32[32]{0:T(128)}, u32[]{:S(2)}) copy-start(s32[32]{0:T(128)} %param.16) | copy-start | bytes 388
  33.3 32.7 %all-to-all-start.2 = ((bf16[32,16,2048]{2,1,0:T(8,128)(2,1)}), bf16[32,16,2048]{2,1,0:T(8,128)(2,1)S(1)}, u32[]{:S(2)}, u32[]{:S(2)}) async-start(bf16[32,16,2048]{2,1,0:T(8,128)(2,1)} %broadcast_select_fusion.1), calls=%async_computation.2 | async-start | bytes 4194304 | tf_op jit(solution)/shard_map/all_to_all | solution.py:68
  37.6 101.7 %all-reduce.2.cloned.1.call-start = ((), (), s32[]{:S(2)}) async-start(), calls=%async_computation.5 | async-start | bytes 212992 | tf_op jit(solution)/shard_map/psum | solution.py:40
  40.0 1.0 copy-start.2
  44.8 25.1 %copy-start.4 = (bf16[128,2048]{1,0:T(8,128)(2,1)S(1)}, bf16[128,2048]{1,0:T(8,128)(2,1)}, u32[]{:S(2)}) copy-start(bf16[128,2048]{1,0:T(8,128)(2,1)} %param.14) | copy-start | bytes 1572868
  104.3 85.9 %all-gather.5.cloned.1.call-start = ((), (), s32[]{:S(2)}) async-start(), calls=%async_computation.6 | async-start | bytes 3514368 | tf_op jit(solution)/shard_map/all_gather | solution.py:41
  139.3 137.7 %all-gather.3.cloned.1.call-start = ((), (), s32[]{:S(2)}) async-start(), calls=%async_computation.4 | async-start | bytes 19021824 | tf_op jit(solution)/shard_map/all_gather | solution.py:32
  277.0 10.5 %copy-start.8 = (bf16[9216,1024]{1,0:T(8,128)(2,1)S(1)}, bf16[9216,1024]{1,0:T(8,128)(2,1)}, u32[]{:S(2)}) copy-start(bf16[9216,1024]{1,0:T(8,128)(2,1)} %all-gather.3.cloned.1.call-done) | copy-start | bytes 56623108
  287.5 7.3 %copy-start.5 = (bf16[128,2048]{1,0:T(8,128)(2,1)S(1)}, bf16[128,2048]{1,0:T(8,128)(2,1)}, u32[]{:S(2)}) copy-start(bf16[128,2048]{1,0:T(8,128)(2,1)} %param.14) | copy-start | bytes 1572868
  303.6 42.9 %all-to-all-start.1 = ((bf16[32,16,2048]{2,1,0:T(8,128)(2,1)}), bf16[32,16,2048]{2,1,0:T(8,128)(2,1)}, u32[]{:S(2)}, u32[]{:S(2)}) async-start(bf16[32,16,2048]{2,1,0:T(8,128)(2,1)} %broadcast_select_fusion), calls=%async_computation.1 | async-start | bytes 4194304 | tf_op jit(solution)/shard_map/all_to_all | solution.py:87
  310.8 22.7 %slice-start = ((s8[4718592]{0:T(1024)(128)(4,1)}), s8[4194304]{0:T(1024)(128)(4,1)S(1)}, s32[]{:S(2)}) async-start(s8[4718592]{0:T(1024)(128)(4,1)} %bitcast.27), calls=%async_computation.7 | async-start | bytes 8388608
  322.2 11.3 %slice-start.1 = ((s8[4718592]{0:T(1024)(128)(4,1)}), s8[524288]{0:T(1024)(128)(4,1)S(1)}, s32[]{:S(2)}) async-start(s8[4718592]{0:T(1024)(128)(4,1)} %bitcast.27), calls=%async_computation.8 | async-start | bytes 1048576
  322.2 11.3 %copy-start.3 = (bf16[4608,128]{1,0:T(8,128)(2,1)S(1)}, bf16[4608,128]{1,0:T(8,128)(2,1)}, u32[]{:S(2)}) copy-start(bf16[4608,128]{1,0:T(8,128)(2,1)} %copy-done.2) | copy-start | bytes 3538948
  341.6 8.2 %copy-start.1 = (bf16[256,2048]{1,0:T(8,128)(2,1)S(1)}, bf16[256,2048]{1,0:T(8,128)(2,1)}, u32[]{:S(2)}) copy-start(bf16[256,2048]{1,0:T(8,128)(2,1)} %param.17) | copy-start | bytes 3145732
Sparse Core Ops, SparseCore 0:
  104.4 34.8 all-reduce.1
  141.8 48.3 all-gather.4
  194.2 82.7 all-gather.2

commit v2 on v1

v2 whole, which is shorter than its diff:
```python
import functools

import jax
import jax.numpy as jnp
from jax import lax
from jax.experimental import pallas as pl
from jax.experimental.pallas import tpu as pltpu
from jax.sharding import Mesh, PartitionSpec as P

DP = ("x", "y", "core")
BF16 = jnp.bfloat16
F32 = jnp.float32
CHUNKS = 2
MIB = 1024 * 1024


def dot(a, b, dims=((1,), (0,))):
    return lax.dot_general(a, b, (dims, ((), ())), preferred_element_type=F32)


def fetch(v, axis, step):
    n = lax.axis_size(axis)
    return lax.ppermute(v, axis, [((i + step) % n, i) for i in range(n)])


def gather_down(down):
    me = lax.axis_index("fsdp")
    rows = down.shape[0]
    full = jnp.zeros((4 * rows, down.shape[1]), down.dtype)
    for step in range(4):
        part = fetch(down, "fsdp", step) if step else down
        full = lax.dynamic_update_slice(full, part, (((me + step) % 4) * rows, 0))
    return full


def far_cut(rows):
    return (rows // 2 + 127) // 128 * 128


def gather_chunk(weight, chunk):
    rows = weight.shape[0]
    cols = weight.shape[1] // CHUNKS
    half = cols // 2
    mine = lax.dynamic_slice(
        weight, (0, chunk * cols + lax.axis_index("core") * half), (rows, half)
    )
    after = fetch(mine, "fsdp", 1)
    before = fetch(mine, "fsdp", 3)
    cut = far_cut(rows)
    far_top = fetch(after[:cut], "fsdp", 1)
    far_low = fetch(before[cut:], "fsdp", 3)
    own = [after, before, far_top, far_low]
    return own + [fetch(p, "core", 1) for p in own]


def sum_scatter(v, axis, wire):
    n = lax.axis_size(axis)
    me = lax.axis_index(axis)
    m = v.shape[0] // n
    total = lax.dynamic_slice_in_dim(v, me * m, m, 0)
    for step in range(1, n):
        part = lax.dynamic_slice_in_dim(v, ((me + n - step) % n) * m, m, 0).astype(wire)
        total = total + fetch(part, axis, step).astype(F32)
    return total


def sum_all(v, axis):
    n = lax.axis_size(axis)
    me = lax.axis_index(axis)
    parts = jnp.zeros((n,) + v.shape, v.dtype)
    for step in range(n):
        part = fetch(v, axis, step) if step else v
        parts = lax.dynamic_update_slice(parts, part[None], ((me + step) % n, 0, 0))
    return jnp.sum(parts, axis=0)


def collect(v, axis):
    n = lax.axis_size(axis)
    me = lax.axis_index(axis)
    m = v.shape[0]
    full = jnp.zeros((n * m, v.shape[1]), v.dtype)
    for step in range(n):
        part = fetch(v, axis, step) if step else v
        full = lax.dynamic_update_slice(full, part, (((me + step) % n) * m, 0))
    return full


def reduce_gradients(grads):
    v = sum_scatter(grads, "core", F32)
    v = sum_scatter(v, "fsdp", BF16)
    v = sum_scatter(v, "x", F32)
    v = sum_all(v, "y").astype(BF16)
    for axis in ("x", "fsdp", "core"):
        v = collect(v, axis)
    return v.astype(F32)


def piece_list(rows):
    cut = far_cut(rows)
    return [(1, 0, rows), (3, 0, rows), (2, 0, cut), (2, cut, rows - cut)]


def forward_kernel(chunk, where, source, xn, low, up, own, *refs):
    pieces, out = refs[:8], refs[8]
    held, own_held, q, sems = refs[9:17], refs[17], refs[18], refs[19]
    me, core = where[0], where[1]
    rows = own.shape[0]
    cols = own_held.shape[1]
    half = cols // 2
    copies = [pltpu.make_async_copy(own.at[:, pl.ds(chunk * cols, cols)], own_held, sems.at[8])]
    copies += [pltpu.make_async_copy(p, h, sems.at[i]) for i, (p, h) in enumerate(zip(pieces, held))]
    for c in copies:
        c.start()
    copies[0].wait()
    for side in range(2):
        at = pl.multiple_of((core if side == 0 else 1 - core) * half, half)
        acc = dot(low[...], up[:, pl.ds(at, half)])
        acc = acc + dot(xn[:, pl.ds(pl.multiple_of(me * rows, 128), rows)], own_held[:, pl.ds(at, half)])
        for i, (shard, first, size) in enumerate(piece_list(rows)):
            copies[1 + side * 4 + i].wait()
            at_row = pl.multiple_of(lax.rem(me + shard, 4) * rows + first, 128)
            acc = acc + dot(xn[:, pl.ds(at_row, size)], held[side * 4 + i][...])
        q[:, pl.ds(at, half)] = acc.astype(BF16)

    def place(d, carry):
        row = pl.multiple_of(source[d] * 16, 16)
        out[pl.ds(pl.multiple_of(d * 16, 16), 16), :] = q[pl.ds(row, 16), :]
        return carry

    lax.fori_loop(0, out.shape[0] // 16, place, 0)


def vmem():
    return pl.BlockSpec(memory_space=pltpu.VMEM)


def smem():
    return pl.BlockSpec(memory_space=pltpu.SMEM)


def anywhere():
    return pl.BlockSpec(memory_space=pl.ANY)


def forward(chunk, where, source, xn, low, up, own, pieces):
    tokens = xn.shape[0]
    cols = own.shape[1] // CHUNKS
    up = up[:, chunk * cols : (chunk + 1) * cols]
    return pl.pallas_call(
        functools.partial(forward_kernel, chunk),
        out_shape=jax.ShapeDtypeStruct((tokens, cols), BF16),
        in_specs=[smem(), smem(), vmem(), vmem(), vmem()] + [anywhere()] * 9,
        out_specs=vmem(),
        scratch_shapes=[pltpu.VMEM(p.shape, BF16) for p in pieces]
        + [
            pltpu.VMEM((own.shape[0], cols), BF16),
            pltpu.VMEM((tokens, cols), BF16),
            pltpu.SemaphoreType.DMA((9,)),
        ],
        compiler_params=pltpu.CompilerParams(vmem_limit_bytes=40 * MIB),
        cost_estimate=pl.CostEstimate(
            flops=2 * tokens * xn.shape[1] * cols, bytes_accessed=16 * MIB, transcendentals=0
        ),
        name="forward",
    )(where, source, xn, low, up, own, *pieces)


def backward_kernel(where, g, dlow, down, x, inverse, gain, live, own, *refs):
    count = 8 * CHUNKS
    pieces, out = refs[:count], refs[count]
    held, own_held, dxn, sems = refs[count + 1 : 2 * count + 1], *refs[2 * count + 1 :]
    me, core = where[0], where[1]
    rows = own.shape[0]
    cols = own.shape[1] // CHUNKS
    half = cols // 2
    copies = [pltpu.make_async_copy(own, own_held, sems.at[count])]
    copies += [pltpu.make_async_copy(p, h, sems.at[i]) for i, (p, h) in enumerate(zip(pieces, held))]
    for c in copies:
        c.start()
    nt = ((1,), (1,))
    tall = g.shape[0]
    base = pl.multiple_of(me * rows, 128)
    copies[0].wait()
    dxn[:, pl.ds(base, rows)] = dot(dlow[...], down[pl.ds(base, rows), :], nt) + dot(g[...], own_held[...], nt)
    for i, (shard, first, size) in enumerate(piece_list(rows)):
        base = pl.multiple_of(lax.rem(me + shard, 4) * rows + first, 128)
        acc = dot(dlow[...], down[pl.ds(base, size), :], nt)
        for chunk in range(CHUNKS):
            for side in range(2):
                n = chunk * 8 + side * 4 + i
                copies[1 + n].wait()
                at = pl.multiple_of(chunk * cols + (core if side == 0 else 1 - core) * half, half)
                acc = acc + dot(g[:, pl.ds(at, half)], held[n][...], nt)
        dxn[:, pl.ds(base, size)] = acc

    def finish(i, carry):
        r = pl.ds(pl.multiple_of(i * 16, 16), 16)
        inv = inverse[r, :]
        dy = dxn[r, :] * gain[...]
        normed = x[r, :].astype(F32) * inv
        mean = jnp.mean(dy * normed, axis=-1, keepdims=True)
        res = jnp.where(live[i] > 0, inv * (dy - normed * mean), 0.0)
        out[r, :] = res.astype(BF16)
        return carry

    lax.fori_loop(0, tall // 16, finish, 0)


def backward(where, g, dlow, down, x, inverse, gain, live, own, pieces):
    tokens, width = x.shape
    return pl.pallas_call(
        backward_kernel,
        out_shape=jax.ShapeDtypeStruct((tokens, width), BF16),
        in_specs=[smem()] + [vmem()] * 6 + [smem()] + [anywhere()] * (1 + len(pieces)),
        out_specs=vmem(),
        scratch_shapes=[pltpu.VMEM(p.shape, BF16) for p in pieces]
        + [
            pltpu.VMEM(own.shape, BF16),
            pltpu.VMEM((tokens, width), F32),
            pltpu.SemaphoreType.DMA((len(pieces) + 1,)),
        ],
        compiler_params=pltpu.CompilerParams(vmem_limit_bytes=56 * MIB),
        cost_estimate=pl.CostEstimate(
            flops=2 * tokens * width * own.shape[1], bytes_accessed=32 * MIB, transcendentals=0
        ),
        name="backward",
    )(where, g, dlow, down, x, inverse, gain, live, own, *pieces)


def body(tokens, gain, weight, down, up, depth, destination, cotangent):
    blocks = depth.shape[0]
    rows, width = tokens.shape
    block_rows = rows // blocks
    features = cotangent.shape[1]
    capacity = cotangent.shape[0] // block_rows
    cols = features // CHUNKS
    live = depth >= 2
    dest = jnp.clip(destination, 0, 31)
    where = jnp.stack([lax.axis_index("fsdp"), lax.axis_index("core")]).astype(jnp.int32)

    hit = live[None, :] & (dest[None, :] == jnp.arange(32, dtype=jnp.int32)[:, None])
    order = jnp.arange(blocks, dtype=jnp.int32)
    source = jnp.sum(jnp.where(hit, order[None, :], 0), axis=1)
    sent = jnp.any(hit, axis=1).astype(jnp.int32)
    flags = lax.all_to_all(sent, DP, 0, 0, tiled=True)
    rank = jnp.sum(jnp.where(order[None, :] < order[:, None], flags[None, :], 0), axis=1)
    seat = jnp.clip(rank, 0, capacity - 1)
    seats = jnp.arange(capacity, dtype=jnp.int32)
    match = (flags[None, :] > 0) & (rank[None, :] == seats[:, None])
    pick = jnp.sum(jnp.where(match, order[None, :], 0), axis=1)

    full_down = gather_down(down)
    pieces = [gather_chunk(weight, chunk) for chunk in range(CHUNKS)]

    g_send = jnp.take(cotangent.reshape(capacity, block_rows, features), seat, axis=0)
    g_got = lax.all_to_all(g_send, DP, 0, 0, tiled=True)
    g = jnp.where(live[:, None, None], jnp.take(g_got, dest, axis=0), jnp.zeros((), BF16))
    g = g.reshape(rows, features)

    x = tokens.astype(F32)
    inverse = lax.rsqrt(jnp.mean(x * x, axis=-1, keepdims=True) + 1e-06)
    gain_f = gain.astype(F32)
    xn = (x * inverse * gain_f).astype(BF16)
    low = dot(xn, full_down).astype(BF16)
    dlow = dot(g, up, ((1,), (1,))).astype(BF16)
    grad_up = dot(low, g, ((0,), (0,)))
    grad_down = dot(xn, dlow, ((0,), (0,)))
    grads = jnp.concatenate([grad_down, grad_up.reshape(-1, grad_down.shape[1])], axis=0)
    grads = reduce_gradients(grads)
    grad_down, grad_up = grads[:width], grads[width:].reshape(grad_up.shape)

    got = []
    for chunk in range(CHUNKS):
        q = forward(chunk, where, source, xn, low, up, weight, pieces[chunk])
        q = lax.all_to_all(q.reshape(blocks, block_rows, cols), DP, 0, 0, tiled=True)
        got.append(jnp.take(q, pick, axis=0).reshape(capacity * block_rows, cols))
    query = jnp.concatenate(got, axis=1)

    grad_tokens = backward(
        where, g, dlow, full_down, tokens, inverse, gain_f.reshape(1, width),
        live.astype(jnp.int32), weight, [p for c in pieces for p in c],
    )
    return query, grad_tokens, grad_down, grad_up


def solution(mesh):
    fine = Mesh(mesh.devices.reshape(4, 4, 2, 4), ("x", "y", "core", "fsdp"))
    split = P(("x", "y", "core", "fsdp"))
    in_specs = (split, P(), P("fsdp"), P("fsdp"), P(), split, split, split)
    return jax.shard_map(
        body, mesh=fine, in_specs=in_specs, out_specs=(split, split, P(), P()), check_vma=False
    )
```

time: 357 us -> 317 us (0.89)
  waiting for transfers between devices: 189 us -> 113 us
  Pallas kernels: 0 us -> 57.4 us
  starting transfers between devices: 25.7 us -> 77.6 us
  matrix products: 58.4 us -> 10.5 us
  blocking collectives: 27.8 us -> 0 us
  between operations: 14.2 us -> 1.6 us
  local copies, waits for them, and re-layouts: 21.6 us -> 28 us
  other arithmetic: 19.5 us -> 24.9 us
    all_gather x2 -> x0, waiting for transfers between devices: 130 us -> none  [the longest x1 81.2 us: gather_weight(): both = lax.all_gather(piece, ('core', 'fsdp', 'x', 'y'), axis=0, tiled=True)]
    ppermute x3 -> x36, waiting for transfers between devices: 0.01 us -> 95.1 us  [fetch(): return lax.ppermute(v, axis, [((i + step) % n, i) for i in range(n)])]
    pallas_call x0 -> x3, Pallas kernels: none -> 57.4 us  [the longest x1 37.9 us: backward(): pl.pallas_call(backward_kernel, out_shape=jax.ShapeDtypeStruct((tokens, w...]
    ppermute x3 -> x36, starting transfers between devices: 5.36 us -> 53.4 us  [fetch(): return lax.ppermute(v, axis, [((i + step) % n, i) for i in range(n)])]
    dot_general x10 -> x4, matrix products: 58.4 us -> 10.5 us  [dot(): return lax.dot_general(a, b, (dims, ((), ())), preferred_element_type=F32)]
    psum x1 -> x0, waiting for transfers between devices: 35 us -> none  [reduce_gradients(): mine = lax.psum(mine, 'fsdp')]
    all_to_all x1 -> x0, blocking collectives: 27.8 us -> none  [reduce_gradients(): parts = lax.all_to_all(grads.astype(BF16), DP, 0, 0, tiled=True)]
    all_to_all x1, waiting for transfers between devices: 21.1 us -> 14.5 us  [body(): g_got = lax.all_to_all(g_send, DP, 0, 0, tiled=True)]
  transfers between devices with their start and end apart: 9 -> 40, of which waited for: 5 -> 16; matrix products, arithmetic and copies ran while one was open for 16% -> 18% of each run, Pallas kernels for 0% -> 18%
where the time goes in v2:
time: 317 us; the launch traced here: 313 us
  waiting for transfers between devices  113 us (36%)
  starting transfers between devices  77.6 us (24%)
  Pallas kernels  57.4 us (18%)
  local copies, waits for them, and re-layouts  28 us (9%)
  other arithmetic  24.9 us (8%)
  matrix products  10.5 us (3%)
    ppermute x36, waiting for transfers between devices, fetch(): return lax.ppermute(v, axis, [((i + step) % n, i) for i in range(n)])  95.1 us
    ppermute x36, starting transfers between devices, fetch(): return lax.ppermute(v, axis, [((i + step) % n, i) for i in range(n)])  53.4 us
    pallas_call x1, Pallas kernels, backward(): pl.pallas_call(backward_kernel, out_shape=jax.ShapeDtypeStruct((tokens, w...  37.9 us
    pallas_call x2, Pallas kernels, forward(): pl.pallas_call(functools.partial(forward_kernel, chunk), out_shape=jax.Sh...  19.6 us
    all_to_all x1, waiting for transfers between devices, body(): g_got = lax.all_to_all(g_send, DP, 0, 0, tiled=True)  14.5 us
    dot_general x4, matrix products, dot(): return lax.dot_general(a, b, (dims, ((), ())), preferred_element_type=F32)  10.5 us
    all_to_all x2, starting transfers between devices, body(): lax.all_to_all(q.reshape(blocks, block_rows, cols), DP, 0, 0, tiled=True)  10.3 us
    all_to_all x1, starting transfers between devices, body(): flags = lax.all_to_all(sent, DP, 0, 0, tiled=True)  8.88 us
  transfers between devices with their start and end apart: 40, of which 16 were waited for; matrix products, arithmetic and copies ran while one was open for 18% of the time, Pallas kernels for 18%

profile of v2, /device:TPU:1, one launch (start us, length us, event | category | flops | bytes accessed | tf_op | source)
XLA Modules:
  0.0 313.0 jit_solution(2016797413899898532)
XLA Ops:
  0.6 4.7 %collective-permute-start = (bf16[1152,128]{1,0:T(8,128)(2,1)}, bf16[1152,128]{1,0:T(8,128)(2,1)}, u32[]{:S(2)}, u32[]{:S(2)}) collective-permute-start(bf16[1152,128]{1,0:T(8,128)(2,1)} %param.13), channel_id=1, source_target_pairs={{1,0},{2,1},{3,2},{0,3},{5,4},{6,5},{7,6},{4,7},{9,8},{10,9},{11,1... | collective-permute-start | bytes 884744 | tf_op jit(solution)/shard_map/ppermute | solution.py:23
  12.7 8.9 %all-to-all-start.1 = ((s32[32,1,1]{2,1,0:T(1,128)}), s32[32,1,1]{2,1,0:T(1,128)S(1)}, u32[]{:S(2)}, u32[]{:S(2)}) async-start(s32[32,1,1]{2,1,0:T(1,128)} %copy.17), calls=%async_computation.1 | async-start | bytes 32768 | tf_op jit(solution)/shard_map/all_to_all | solution.py:245
  21.7 3.3 %fusion = f32[512]{0:T(512)S(1)} fusion(bf16[512,4608]{1,0:T(8,128)(2,1)} %x.1), kind=kLoop, calls=%fused_computation.6 | loop fusion | flops 7077376 | bytes 4720640 | tf_op jit(solution)/shard_map/reduce_sum | solution.py:261
  25.1 3.4 %all-to-all-done.1 = s32[32,1,1]{2,1,0:T(1,128)S(1)} async-done(((s32[32,1,1]{2,1,0:T(1,128)}), s32[32,1,1]{2,1,0:T(1,128)S(1)}, u32[]{:S(2)}, u32[]{:S(2)}) %all-to-all-start.1) | async-done | bytes 160 | tf_op jit(solution)/shard_map/all_to_all | solution.py:245
  31.6 5.0 %all-to-all-start.3 = ((bf16[32,16,2048]{2,1,0:T(8,128)(2,1)}), bf16[32,16,2048]{2,1,0:T(8,128)(2,1)}, u32[]{:S(2)}, u32[]{:S(2)}) async-start(bf16[32,16,2048]{2,1,0:T(8,128)(2,1)} %broadcast_select_fusion), calls=%async_computation.3 | async-start | bytes 4194304 | tf_op jit(solution)/shard_map/all_to_all | solution.py:256
  36.6 6.1 %fusion.2.xn = bf16[512,4608]{1,0:T(8,128)(2,1)} fusion(bf16[512,4608]{1,0:T(8,128)(2,1)} %x.1, f32[4608]{0:T(1024)S(1)} %convert_element_type.56, f32[512]{0:T(512)S(1)} %add_rsqrt_fusion), kind=kLoop, calls=%fused_computation.8 | loop fusion | flops 9437184 | bytes 9457664 | tf_op jit(solution)/shard_map/convert_element_type | solution.py:263
  46.4 4.1 %fusion.15.low = bf16[512,128]{1,0:T(8,128)(2,1)S(1)} fusion(bf16[512,4608]{1,0:T(8,128)(2,1)} %fusion.2.xn, bf16[4608,128]{1,0:T(8,128)(2,1)S(1)} %constant_dynamic-update-slice_fusion.10.down), kind=kOutput, calls=%fused_computation.81 | convolution fusion | flops 603979776 | bytes 6029312 | tf_op jit(solution)/shard_map/dot_general | solution.py:18
  50.5 14.5 %all-to-all-done.3 = bf16[32,16,2048]{2,1,0:T(8,128)(2,1)} async-done(((bf16[32,16,2048]{2,1,0:T(8,128)(2,1)}), bf16[32,16,2048]{2,1,0:T(8,128)(2,1)}, u32[]{:S(2)}, u32[]{:S(2)}) %all-to-all-start.3) | async-done | bytes 2097184 | tf_op jit(solution)/shard_map/all_to_all | solution.py:256
  69.8 5.2 %fusion.16 = f32[4608,128]{1,0:T(8,128)} fusion(bf16[512,4608]{1,0:T(8,128)(2,1)} %fusion.2.xn, bf16[512,128]{1,0:T(8,128)(2,1)S(1)} %convolution_convert_fusion.dlow), kind=kOutput, calls=%fused_computation.82 | convolution fusion | flops 603979776 | bytes 7208960 | tf_op jit(solution)/shard_map/dot_general | solution.py:18
  89.9 17.6 %collective-permute-done.3.refs_0_ = bf16[1152,512]{1,0:T(8,128)(2,1)S(1)} collective-permute-done((bf16[1152,512]{1,0:T(8,128)(2,1)}, bf16[1152,512]{1,0:T(8,128)(2,1)S(1)}, u32[]{:S(2)}, u32[]{:S(2)}) %collective-permute-start.3) | collective-permute-done | bytes 1179680 | tf_op jit(solution)/shard_map/ppermute | solution.py:23
  110.6 22.0 %collective-permute-done.11.refs_0_.refs_8_ = bf16[1152,512]{1,0:T(8,128)(2,1)S(1)} collective-permute-done((bf16[1152,512]{1,0:T(8,128)(2,1)}, bf16[1152,512]{1,0:T(8,128)(2,1)S(1)}, u32[]{:S(2)}, u32[]{:S(2)}) %collective-permute-start.11) | collective-permute-done | bytes 1179680 | tf_op jit(solution)/shard_map/ppermute | solution.py:23
  140.4 6.3 %collective-permute-done.5.refs_2_ = bf16[640,512]{1,0:T(8,128)(2,1)S(1)} collective-permute-done((bf16[640,512]{1,0:T(8,128)(2,1)S(1)}, bf16[640,512]{1,0:T(8,128)(2,1)S(1)}, u32[]{:S(2)}, u32[]{:S(2)}) %collective-permute-start.5) | collective-permute-done | bytes 655392 | tf_op jit(solution)/shard_map/ppermute | solution.py:23
  146.7 14.1 %collective-permute-done.13.refs_2_.refs_10_ = bf16[640,512]{1,0:T(8,128)(2,1)} collective-permute-done((bf16[640,512]{1,0:T(8,128)(2,1)S(1)}, bf16[640,512]{1,0:T(8,128)(2,1)}, u32[]{:S(2)}, u32[]{:S(2)}) %collective-permute-start.13) | collective-permute-done | bytes 655392 | tf_op jit(solution)/shard_map/ppermute | solution.py:23
  170.0 3.6 %collective-permute-done.20 = bf16[832,128]{1,0:T(8,128)(2,1)S(1)} collective-permute-done((bf16[832,128]{1,0:T(8,128)(2,1)S(1)}, bf16[832,128]{1,0:T(8,128)(2,1)S(1)}, u32[]{:S(2)}, u32[]{:S(2)}) %collective-permute-start.20) | collective-permute-done | bytes 213024 | tf_op jit(solution)/shard_map/ppermute | solution.py:23
  177.9 6.5 %collective-permute-done.25 = f32[208,128]{1,0:T(8,128)} collective-permute-done((f32[208,128]{1,0:T(8,128)S(1)}, f32[208,128]{1,0:T(8,128)}, u32[]{:S(2)}, u32[]{:S(2)}) %collective-permute-start.25) | collective-permute-done | bytes 106528 | tf_op jit(solution)/shard_map/ppermute | solution.py:23
  185.3 9.8 %forward.2 = bf16[512,1024]{1,0:T(8,128)(2,1)} custom-call(s32[2]{0:T(128)S(1)} %pad_add_fusion.where, s32[32]{0:T(128)S(1)} %select_reduce_fusion.1.source, bf16[512,4608]{1,0:T(8,128)(2,1)S(1)} %bitcast.36, bf16[512,128]{1,0:T(8,128)(2,1)S(1)} %fusion.15.low, bf16[128,1024]{1,0:T(8,128)(2,1)S(1)} %get-tuple-element.14.up, bf16[1152,2048]{1,0:T(8,128)(2,1)} %own.5, ...), custom_call_target="tpu_custom_call" | custom-call | flops 4831838208 | bytes 16777216 | tf_op jit(solution)/shard_map/forward/pallas_call | solution.py:149
  195.1 4.7 %all-to-all-start = ((bf16[32,16,1024]{2,1,0:T(8,128)(2,1)}), bf16[32,16,1024]{2,1,0:T(8,128)(2,1)S(1)}, u32[]{:S(2)}, u32[]{:S(2)}) async-start(bf16[32,16,1024]{2,1,0:T(8,128)(2,1)} %bitcast.3), calls=%async_computation | async-start | bytes 2097152 | tf_op jit(solution)/shard_map/all_to_all | solution.py:275
  202.3 14.5 %collective-permute-start.26 = (f32[208,128]{1,0:T(8,128)S(1)}, f32[208,128]{1,0:T(8,128)S(1)}, u32[]{:S(2)}, u32[]{:S(2)}) collective-permute-start(f32[208,128]{1,0:T(8,128)S(1)} %get-tuple-element.6), channel_id=1, source_target_pairs={{8,0},{16,8},{24,16},{0,24},{9,1},{17,9},{25,17},{1,25},{10,2},{18... | collective-permute-start | bytes 319496 | tf_op jit(solution)/shard_map/ppermute | solution.py:23
  219.2 9.8 %forward.3 = bf16[512,1024]{1,0:T(8,128)(2,1)} custom-call(s32[2]{0:T(128)S(1)} %pad_add_fusion.where, s32[32]{0:T(128)S(1)} %select_reduce_fusion.1.source, bf16[512,4608]{1,0:T(8,128)(2,1)S(1)} %copy-done.2, bf16[512,128]{1,0:T(8,128)(2,1)S(1)} %fusion.15.low, bf16[128,1024]{1,0:T(8,128)(2,1)S(1)} %copy-done.7, bf16[1152,2048]{1,0:T(8,128)(2,1)} %own.5, ...), custom_call_target="tpu_custom_call" | custom-call | flops 4831838208 | bytes 16777216 | tf_op jit(solution)/shard_map/forward/pallas_call | solution.py:149
  230.9 3.6 %collective-permute-done.27 = f32[208,128]{1,0:T(8,128)S(1)} collective-permute-done((f32[208,128]{1,0:T(8,128)S(1)}, f32[208,128]{1,0:T(8,128)S(1)}, u32[]{:S(2)}, u32[]{:S(2)}) %collective-permute-start.27) | collective-permute-done | bytes 106528 | tf_op jit(solution)/shard_map/ppermute | solution.py:23
  246.5 5.6 %all-to-all-start.2 = ((bf16[32,16,1024]{2,1,0:T(8,128)(2,1)}), bf16[32,16,1024]{2,1,0:T(8,128)(2,1)S(1)}, u32[]{:S(2)}, u32[]{:S(2)}) async-start(bf16[32,16,1024]{2,1,0:T(8,128)(2,1)} %bitcast.5), calls=%async_computation.2 | async-start | bytes 2097152 | tf_op jit(solution)/shard_map/all_to_all | solution.py:275
  254.3 37.9 %backward.1 = bf16[512,4608]{1,0:T(8,128)(2,1)} custom-call(s32[2]{0:T(128)} %copy-done.12, bf16[512,2048]{1,0:T(8,128)(2,1)} %copy-done.14, bf16[512,128]{1,0:T(8,128)(2,1)} %copy-done.20, bf16[4608,128]{1,0:T(8,128)(2,1)} %copy-done.19, bf16[512,4608]{1,0:T(8,128)(2,1)} %x.1, f32[512,1]{1,0:T(8,128)} %copy.18.inverse, f32[1,4608]{1,0:T(1,128)} %broadcast_in_dim.144.gain, ...), custom_call_target="tpu_custom_call" | custom-call | flops 9663676416 | bytes 33554432 | tf_op jit(solution)/shard_map/backward/pallas_call | solution.py:211
  295.1 6.9 %collective-permute-done.33 = bf16[832,128]{1,0:T(8,128)(2,1)S(1)} collective-permute-done((bf16[832,128]{1,0:T(8,128)(2,1)S(1)}, bf16[832,128]{1,0:T(8,128)(2,1)S(1)}, u32[]{:S(2)}, u32[]{:S(2)}) %collective-permute-start.33) | collective-permute-done | bytes 213024 | tf_op jit(solution)/shard_map/ppermute | solution.py:23
  302.1 5.0 %collective-permute-done.34 = bf16[832,128]{1,0:T(8,128)(2,1)S(1)} collective-permute-done((bf16[832,128]{1,0:T(8,128)(2,1)S(1)}, bf16[832,128]{1,0:T(8,128)(2,1)S(1)}, u32[]{:S(2)}, u32[]{:S(2)}) %collective-permute-start.34) | collective-permute-done | bytes 213024 | tf_op jit(solution)/shard_map/ppermute | solution.py:23
  (201 shorter events, 88.2 us)
Async XLA Ops:
  0.6 42.6 %collective-permute-start = (bf16[1152,128]{1,0:T(8,128)(2,1)}, bf16[1152,128]{1,0:T(8,128)(2,1)}, u32[]{:S(2)}, u32[]{:S(2)}) collective-permute-start(bf16[1152,128]{1,0:T(8,128)(2,1)} %param.13), channel_id=1, source_target_pairs={{1,0},{2,1},{3,2},{0,3},{5,4},{6,5},{7,6},{4,7},{9,8},{10,9},{11,1... | collective-permute-start | bytes 884744 | tf_op jit(solution)/shard_map/ppermute | solution.py:23
  5.3 39.0 %collective-permute-start.1 = (bf16[1152,128]{1,0:T(8,128)(2,1)}, bf16[1152,128]{1,0:T(8,128)(2,1)}, u32[]{:S(2)}, u32[]{:S(2)}) collective-permute-start(bf16[1152,128]{1,0:T(8,128)(2,1)} %param.13), channel_id=1, source_target_pairs={{2,0},{3,1},{0,2},{1,3},{6,4},{7,5},{4,6},{5,7},{10,8},{11,9},{8,1... | collective-permute-start | bytes 884744 | tf_op jit(solution)/shard_map/ppermute | solution.py:23
  5.3 40.0 %collective-permute-start.2 = (bf16[1152,128]{1,0:T(8,128)(2,1)}, bf16[1152,128]{1,0:T(8,128)(2,1)}, u32[]{:S(2)}, u32[]{:S(2)}) collective-permute-start(bf16[1152,128]{1,0:T(8,128)(2,1)} %param.13), channel_id=1, source_target_pairs={{3,0},{0,1},{1,2},{2,3},{7,4},{4,5},{5,6},{6,7},{11,8},{8,9},{9,10... | collective-permute-start | bytes 884744 | tf_op jit(solution)/shard_map/ppermute | solution.py:23
  9.3 74.6 %collective-permute-start.4 = (bf16[1152,512]{1,0:T(8,128)(2,1)}, bf16[1152,512]{1,0:T(8,128)(2,1)}, u32[]{:S(2)}, u32[]{:S(2)}) collective-permute-start(bf16[1152,512]{1,0:T(8,128)(2,1)} %get-tuple-element.9), channel_id=1, source_target_pairs={{3,0},{0,1},{1,2},{2,3},{7,4},{4,5},{5,6},{6,7},{11,8},{8,9},{9,10... | collective-permute-start | bytes 3538952 | tf_op jit(solution)/shard_map/ppermute | solution.py:23
  21.6 65.0 %collective-permute-start.12 = (bf16[1152,512]{1,0:T(8,128)(2,1)}, bf16[1152,512]{1,0:T(8,128)(2,1)}, u32[]{:S(2)}, u32[]{:S(2)}) collective-permute-start(bf16[1152,512]{1,0:T(8,128)(2,1)} %get-tuple-element.10), channel_id=1, source_target_pairs={{3,0},{0,1},{1,2},{2,3},{7,4},{4,5},{5,6},{6,7},{11,8},{8,9},{9,10... | collective-permute-start | bytes 3538952 | tf_op jit(solution)/shard_map/ppermute | solution.py:23
  31.6 33.4 %all-to-all-start.3 = ((bf16[32,16,2048]{2,1,0:T(8,128)(2,1)}), bf16[32,16,2048]{2,1,0:T(8,128)(2,1)}, u32[]{:S(2)}, u32[]{:S(2)}) async-start(bf16[32,16,2048]{2,1,0:T(8,128)(2,1)} %broadcast_select_fusion), calls=%async_computation.3 | async-start | bytes 4194304 | tf_op jit(solution)/shard_map/all_to_all | solution.py:256
  78.9 58.7 %collective-permute-start.19 = (f32[3328,128]{1,0:T(8,128)}, f32[3328,128]{1,0:T(8,128)}, u32[]{:S(2)}, u32[]{:S(2)}) collective-permute-start(f32[3328,128]{1,0:T(8,128)} %fusion.6), channel_id=1, source_target_pairs={{4,0},{0,4},{5,1},{1,5},{6,2},{2,6},{7,3},{3,7},{12,8},{8,12},{13,... | collective-permute-start | bytes 5111816 | tf_op jit(solution)/shard_map/ppermute | solution.py:23
  79.6 27.9 %collective-permute-start.3 = (bf16[1152,512]{1,0:T(8,128)(2,1)}, bf16[1152,512]{1,0:T(8,128)(2,1)S(1)}, u32[]{:S(2)}, u32[]{:S(2)}) collective-permute-start(bf16[1152,512]{1,0:T(8,128)(2,1)} %get-tuple-element.9), channel_id=1, source_target_pairs={{1,0},{2,1},{3,2},{0,3},{5,4},{6,5},{7,6},{4,7},{9,8},{10,9},{11,1... | collective-permute-start | bytes 3538952 | tf_op jit(solution)/shard_map/ppermute | solution.py:23
  81.5 51.1 %collective-permute-start.11 = (bf16[1152,512]{1,0:T(8,128)(2,1)}, bf16[1152,512]{1,0:T(8,128)(2,1)S(1)}, u32[]{:S(2)}, u32[]{:S(2)}) collective-permute-start(bf16[1152,512]{1,0:T(8,128)(2,1)} %get-tuple-element.10), channel_id=1, source_target_pairs={{1,0},{2,1},{3,2},{0,3},{5,4},{6,5},{7,6},{4,7},{9,8},{10,9},{11,1... | collective-permute-start | bytes 3538952 | tf_op jit(solution)/shard_map/ppermute | solution.py:23
  85.0 50.8 %collective-permute-start.6 = (bf16[512,512]{1,0:T(8,128)(2,1)S(1)}, bf16[512,512]{1,0:T(8,128)(2,1)S(1)}, u32[]{:S(2)}, u32[]{:S(2)}) collective-permute-start(bf16[512,512]{1,0:T(8,128)(2,1)S(1)} %slice.41), channel_id=1, source_target_pairs={{3,0},{0,1},{1,2},{2,3},{7,4},{4,5},{5,6},{6,7},{11,8},{8,9},{9,10... | collective-permute-start | bytes 1572872 | tf_op jit(solution)/shard_map/ppermute | solution.py:23
  87.6 49.8 %collective-permute-start.14 = (bf16[512,512]{1,0:T(8,128)(2,1)S(1)}, bf16[512,512]{1,0:T(8,128)(2,1)}, u32[]{:S(2)}, u32[]{:S(2)}) collective-permute-start(bf16[512,512]{1,0:T(8,128)(2,1)S(1)} %slice.43), channel_id=1, source_target_pairs={{3,0},{0,1},{1,2},{2,3},{7,4},{4,5},{5,6},{6,7},{11,8},{8,9},{9,10... | collective-permute-start | bytes 1572872 | tf_op jit(solution)/shard_map/ppermute | solution.py:23
  107.5 39.2 %collective-permute-start.5 = (bf16[640,512]{1,0:T(8,128)(2,1)S(1)}, bf16[640,512]{1,0:T(8,128)(2,1)S(1)}, u32[]{:S(2)}, u32[]{:S(2)}) collective-permute-start(bf16[640,512]{1,0:T(8,128)(2,1)S(1)} %slice.40), channel_id=1, source_target_pairs={{1,0},{2,1},{3,2},{0,3},{5,4},{6,5},{7,6},{4,7},{9,8},{10,9},{11,1... | collective-permute-start | bytes 1966088 | tf_op jit(solution)/shard_map/ppermute | solution.py:23
  132.7 28.1 %collective-permute-start.13 = (bf16[640,512]{1,0:T(8,128)(2,1)S(1)}, bf16[640,512]{1,0:T(8,128)(2,1)}, u32[]{:S(2)}, u32[]{:S(2)}) collective-permute-start(bf16[640,512]{1,0:T(8,128)(2,1)S(1)} %slice.42), channel_id=1, source_target_pairs={{1,0},{2,1},{3,2},{0,3},{5,4},{6,5},{7,6},{4,7},{9,8},{10,9},{11,1... | collective-permute-start | bytes 1966088 | tf_op jit(solution)/shard_map/ppermute | solution.py:23
  135.9 40.3 %collective-permute-start.7 = (bf16[1152,512]{1,0:T(8,128)(2,1)S(1)}, bf16[1152,512]{1,0:T(8,128)(2,1)S(1)}, u32[]{:S(2)}, u32[]{:S(2)}) collective-permute-start(bf16[1152,512]{1,0:T(8,128)(2,1)S(1)} %collective-permute-done.3.refs_0_), channel_id=1, source_target_pairs={{4,0},{0,4},{5,1},{1,5},{6,2},{2,6},{7,3},{3,7},{12,8},{8,12},{13,... | collective-permute-start | bytes 3538952 | tf_op jit(solution)/shard_map/ppermute | solution.py:23
  137.5 38.7 %collective-permute-start.8 = (bf16[1152,512]{1,0:T(8,128)(2,1)}, bf16[1152,512]{1,0:T(8,128)(2,1)S(1)}, u32[]{:S(2)}, u32[]{:S(2)}) collective-permute-start(bf16[1152,512]{1,0:T(8,128)(2,1)} %collective-permute-done.4.refs_1_), channel_id=1, source_target_pairs={{4,0},{0,4},{5,1},{1,5},{6,2},{2,6},{7,3},{3,7},{12,8},{8,12},{13,... | collective-permute-start | bytes 3538952 | tf_op jit(solution)/shard_map/ppermute | solution.py:23
  137.6 25.0 %collective-permute-start.10 = (bf16[512,512]{1,0:T(8,128)(2,1)S(1)}, bf16[512,512]{1,0:T(8,128)(2,1)S(1)}, u32[]{:S(2)}, u32[]{:S(2)}) collective-permute-start(bf16[512,512]{1,0:T(8,128)(2,1)S(1)} %collective-permute-done.6.refs_3_), channel_id=1, source_target_pairs={{4,0},{0,4},{5,1},{1,5},{6,2},{2,6},{7,3},{3,7},{12,8},{8,12},{13,... | collective-permute-start | bytes 1572872 | tf_op jit(solution)/shard_map/ppermute | solution.py:23
  164.0 52.8 %collective-permute-start.15 = (bf16[1152,512]{1,0:T(8,128)(2,1)S(1)}, bf16[1152,512]{1,0:T(8,128)(2,1)}, u32[]{:S(2)}, u32[]{:S(2)}) collective-permute-start(bf16[1152,512]{1,0:T(8,128)(2,1)S(1)} %collective-permute-done.11.refs_0_.refs_8_), channel_id=1, source_target_pairs={{4,0},{0,4},{5,1},{1,5},{6,2},{2,6},{7,3},{3,7},{12,8},{8,12},{13,... | collective-permute-start | bytes 3538952 | tf_op jit(solution)/shard_map/ppermute | solution.py:23
  168.2 48.6 %collective-permute-start.16 = (bf16[1152,512]{1,0:T(8,128)(2,1)}, bf16[1152,512]{1,0:T(8,128)(2,1)}, u32[]{:S(2)}, u32[]{:S(2)}) collective-permute-start(bf16[1152,512]{1,0:T(8,128)(2,1)} %collective-permute-done.12.refs_1_.refs_9_), channel_id=1, source_target_pairs={{4,0},{0,4},{5,1},{1,5},{6,2},{2,6},{7,3},{3,7},{12,8},{8,12},{13,... | collective-permute-start | bytes 3538952 | tf_op jit(solution)/shard_map/ppermute | solution.py:23
  177.2 39.6 %collective-permute-start.18 = (bf16[512,512]{1,0:T(8,128)(2,1)}, bf16[512,512]{1,0:T(8,128)(2,1)}, u32[]{:S(2)}, u32[]{:S(2)}) collective-permute-start(bf16[512,512]{1,0:T(8,128)(2,1)} %collective-permute-done.14.refs_3_.refs_11_), channel_id=1, source_target_pairs={{4,0},{0,4},{5,1},{1,5},{6,2},{2,6},{7,3},{3,7},{12,8},{8,12},{13,... | collective-permute-start | bytes 1572872 | tf_op jit(solution)/shard_map/ppermute | solution.py:23
  184.4 32.4 %collective-permute-start.17 = (bf16[640,512]{1,0:T(8,128)(2,1)}, bf16[640,512]{1,0:T(8,128)(2,1)}, u32[]{:S(2)}, u32[]{:S(2)}) collective-permute-start(bf16[640,512]{1,0:T(8,128)(2,1)} %collective-permute-done.13.refs_2_.refs_10_), channel_id=1, source_target_pairs={{4,0},{0,4},{5,1},{1,5},{6,2},{2,6},{7,3},{3,7},{12,8},{8,12},{13,... | collective-permute-start | bytes 1966088 | tf_op jit(solution)/shard_map/ppermute | solution.py:23
  195.1 51.4 %all-to-all-start = ((bf16[32,16,1024]{2,1,0:T(8,128)(2,1)}), bf16[32,16,1024]{2,1,0:T(8,128)(2,1)S(1)}, u32[]{:S(2)}, u32[]{:S(2)}) async-start(bf16[32,16,1024]{2,1,0:T(8,128)(2,1)} %bitcast.3), calls=%async_computation | async-start | bytes 2097152 | tf_op jit(solution)/shard_map/all_to_all | solution.py:275
  202.3 27.9 %collective-permute-start.26 = (f32[208,128]{1,0:T(8,128)S(1)}, f32[208,128]{1,0:T(8,128)S(1)}, u32[]{:S(2)}, u32[]{:S(2)}) collective-permute-start(f32[208,128]{1,0:T(8,128)S(1)} %get-tuple-element.6), channel_id=1, source_target_pairs={{8,0},{16,8},{24,16},{0,24},{9,1},{17,9},{25,17},{1,25},{10,2},{18... | collective-permute-start | bytes 319496 | tf_op jit(solution)/shard_map/ppermute | solution.py:23
  246.5 47.1 %all-to-all-start.2 = ((bf16[32,16,1024]{2,1,0:T(8,128)(2,1)}), bf16[32,16,1024]{2,1,0:T(8,128)(2,1)S(1)}, u32[]{:S(2)}, u32[]{:S(2)}) async-start(bf16[32,16,1024]{2,1,0:T(8,128)(2,1)} %bitcast.5), calls=%async_computation.2 | async-start | bytes 2097152 | tf_op jit(solution)/shard_map/all_to_all | solution.py:275
  252.1 42.9 %collective-permute-start.32 = (bf16[832,128]{1,0:T(8,128)(2,1)S(1)}, bf16[832,128]{1,0:T(8,128)(2,1)S(1)}, u32[]{:S(2)}, u32[]{:S(2)}) collective-permute-start(bf16[832,128]{1,0:T(8,128)(2,1)S(1)} %constant_dynamic-update-slice_fusion.6), channel_id=1, source_target_pairs={{1,0},{2,1},{3,2},{0,3},{5,4},{6,5},{7,6},{4,7},{9,8},{10,9},{11,1... | collective-permute-start | bytes 638984 | tf_op jit(solution)/shard_map/ppermute | solution.py:23
  (47 other events, 909.3 us)

commit v3 on v1

--- a/solution.py
+++ b/solution.py
@@ -1,15 +1,24 @@
 import jax
 import jax.numpy as jnp
 from jax import lax
+from jax.experimental import pallas as pl
+from jax.experimental.pallas import tpu as pltpu
 from jax.sharding import Mesh, PartitionSpec as P
 
 DP = ("x", "y", "core")
 BF16 = jnp.bfloat16
 F32 = jnp.float32
+CHUNKS = 2
+MIB = 1024 * 1024
 
 
 def dot(a, b, dims=((1,), (0,))):
     return lax.dot_general(a, b, (dims, ((), ())), preferred_element_type=F32)
+
+
+def fetch(v, axis, step):
+    n = lax.axis_size(axis)
+    return lax.ppermute(v, axis, [((i + step) % n, i) for i in range(n)])
 
 
 def gather_down(down):
@@ -17,9 +26,7 @@
     rows = down.shape[0]
     full = jnp.zeros((4 * rows, down.shape[1]), down.dtype)
     for step in range(4):
-        part = down
-        if step:
-            part = lax.ppermute(down, "fsdp", [((i + step) % 4, i) for i in range(4)])
+        part = fetch(down, "fsdp", step) if step else down
         full = lax.dynamic_update_slice(full, part, (((me + step) % 4) * rows, 0))
     return full
 
@@ -33,12 +40,141 @@
     return both.reshape(2, both.shape[0] // 2, half)
 
 
+def sum_scatter(v, axis, wire):
+    n = lax.axis_size(axis)
+    me = lax.axis_index(axis)
+    m = v.shape[0] // n
+    total = lax.dynamic_slice_in_dim(v, me * m, m, 0)
+    for step in range(1, n):
+        part = lax.dynamic_slice_in_dim(v, ((me + n - step) % n) * m, m, 0).astype(wire)
+        total = total + fetch(part, axis, step).astype(F32)
+    return total
+
+
+def sum_all(v, axis):
+    n = lax.axis_size(axis)
+    me = lax.axis_index(axis)
+    parts = jnp.zeros((n,) + v.shape, v.dtype)
+    for step in range(n):
+        part = fetch(v, axis, step) if step else v
+        parts = lax.dynamic_update_slice(parts, part[None], ((me + step) % n, 0, 0))
+    return jnp.sum(parts, axis=0)
+
+
+def collect(v, axis):
+    n = lax.axis_size(axis)
+    me = lax.axis_index(axis)
+    m = v.shape[0]
+    full = jnp.zeros((n * m, v.shape[1]), v.dtype)
+    for step in range(n):
+        part = fetch(v, axis, step) if step else v
+        full = lax.dynamic_update_slice(full, part, (((me + step) % n) * m, 0))
+    return full
+
+
 def reduce_gradients(grads):
-    rows, lanes = grads.shape
-    parts = lax.all_to_all(grads.astype(BF16), DP, 0, 0, tiled=True)
-    mine = jnp.sum(parts.reshape(32, rows // 32, lanes).astype(F32), axis=0)
-    mine = lax.psum(mine, "fsdp")
-    return lax.all_gather(mine, DP, axis=0, tiled=True)
+    v = sum_scatter(grads, "core", F32)
+    v = sum_scatter(v, "fsdp", BF16)
+    v = sum_scatter(v, "x", F32)
+    v = sum_all(v, "y").astype(BF16)
+    for axis in ("x", "fsdp", "core"):
+        v = collect(v, axis)
+    return v.astype(F32)
+
+
+def forward_kernel(source, xn, low, w, up, out, q):
+    q[...] = (dot(xn[...], w[0]) + dot(low[...], up[...])).astype(BF16)
+
+    def place(d, carry):
+        row = pl.multiple_of(source[d] * 16, 16)
+        out[pl.ds(pl.multiple_of(d * 16, 16), 16), :] = q[pl.ds(row, 16), :]
+        return carry
+
+    lax.fori_loop(0, out.shape[0] // 16, place, 0)
+
+
+def forward(chunk, source, xn, low, w, up):
+    tokens, width = xn.shape
+    cols = w.shape[2]
+    tile = 512
+    base = chunk * (cols // tile)
+    return pl.pallas_call(
+        forward_kernel,
+        out_shape=jax.ShapeDtypeStruct((tokens, cols), BF16),
+        grid_spec=pltpu.PrefetchScalarGridSpec(
+            num_scalar_prefetch=1,
+            grid=(cols // tile,),
+            in_specs=[
+                pl.BlockSpec((tokens, width), lambda i, s: (0, 0)),
+                pl.BlockSpec(low.shape, lambda i, s: (0, 0)),
+                pl.BlockSpec((1, width, tile), lambda i, s: (chunk, 0, i)),
+                pl.BlockSpec((up.shape[0], tile), lambda i, s: (0, base + i)),
+            ],
+            out_specs=pl.BlockSpec((tokens, tile), lambda i, s: (0, i)),
+            scratch_shapes=[pltpu.VMEM((tokens, tile), BF16)],
+        ),
+        compiler_params=pltpu.CompilerParams(vmem_limit_bytes=40 * MIB),
+        cost_estimate=pl.CostEstimate(
+            flops=2 * tokens * width * cols, bytes_accessed=16 * MIB, transcendentals=0
+        ),
+        name="forward",
+    )(source, xn, low, w, up)
+
+
+def backward_kernel(live, g, dlow, w, down, x, gain, inverse, out, dxn):
+    i = pl.program_id(0)
+    nt = ((1,), (1,))
+    half = w.shape[2]
+    tile = w.shape[1]
+    acc = dot(g[:, :half], w[0], nt) + dot(g[:, half:], w[1], nt) + dot(dlow[...], down[...], nt)
+    dxn[:, pl.ds(pl.multiple_of(i * tile, tile), tile)] = acc
+
+    @pl.when(i == pl.num_programs(0) - 1)
+    def _():
+        def finish(j, carry):
+            r = pl.ds(pl.multiple_of(j * 16, 16), 16)
+            inv = inverse[r, :]
+            dy = dxn[r, :] * gain[...]
+            normed = x[r, :].astype(F32) * inv
+            mean = jnp.mean(dy * normed, axis=-1, keepdims=True)
+            res = jnp.where(live[j] > 0, inv * (dy - normed * mean), 0.0)
+            out[r, :] = res.astype(BF16)
+            return carry
+
+        lax.fori_loop(0, x.shape[0] // 16, finish, 0)
+
+
+def backward(live, g, dlow, w, down, x, gain, inverse):
+    tokens, width = x.shape
+    tile = 512
+
+    def whole(v):
+        return pl.BlockSpec(v.shape, lambda i, s: (0, 0))
+
+    return pl.pallas_call(
+        backward_kernel,
+        out_shape=jax.ShapeDtypeStruct((tokens, width), BF16),
+        grid_spec=pltpu.PrefetchScalarGridSpec(
+            num_scalar_prefetch=1,
+            grid=(width // tile,),
+            in_specs=[
+                whole(g),
+                whole(dlow),
+                pl.BlockSpec((2, tile, w.shape[2]), lambda i, s: (0, i, 0)),
+                pl.BlockSpec((tile, down.shape[1]), lambda i, s: (i, 0)),
+                whole(x),
+                whole(gain),
+                whole(inverse),
+            ],
+            out_specs=whole(x),
+            scratch_shapes=[pltpu.VMEM((tokens, width), F32)],
+        ),
+        compiler_params=pltpu.CompilerParams(vmem_limit_bytes=56 * MIB),
+        cost_estimate=pl.CostEstimate(
+            flops=2 * tokens * width * g.shape[1], bytes_accessed=32 * MIB, transcendentals=0
+        ),
+        name="backward",
+    )(live, g, dlow, w, down, x, gain, inverse)
 
 
 def body(tokens, gain, weight, down, up, depth, destination, cotangent):
@@ -47,6 +183,7 @@
     block_rows = rows // blocks
     features = cotangent.shape[1]
     capacity = cotangent.shape[0] // block_rows
+    cols = features // CHUNKS
     live = depth >= 2
     dest = jnp.clip(destination, 0, 31)
 
@@ -61,8 +198,8 @@
     match = (flags[None, :] > 0) & (rank[None, :] == seats[:, None])
     pick = jnp.sum(jnp.where(match, order[None, :], 0), axis=1)
 
+    full_down = gather_down(down)
     full_weight = gather_weight(weight)
-    full_down = gather_down(down)
 
     g_send = jnp.take(cotangent.reshape(capacity, block_rows, features), seat, axis=0)
     g_got = lax.all_to_all(g_send, DP, 0, 0, tiled=True)
@@ -81,18 +218,16 @@
     grads = reduce_gradients(grads)
     grad_down, grad_up = grads[:width], grads[width:].reshape(grad_up.shape)
 
-    half = features // 2
-    q = jnp.concatenate([dot(xn, full_weight[0]), dot(xn, full_weight[1])], axis=1)
-    q = (q + dot(low, up)).astype(BF16).reshape(blocks, block_rows, features)
-    q_got = lax.all_to_all(jnp.take(q, source, axis=0), DP, 0, 0, tiled=True)
-    query = jnp.take(q_got, pick, axis=0).reshape(capacity * block_rows, features)
-
-    dxn = dot(g[:, :half], full_weight[0], ((1,), (1,))) + dot(g[:, half:], full_weight[1], ((1,), (1,)))
-    dxn = dxn + dot(dlow, full_down, ((1,), (1,)))
-    dy = dxn * gain_f
-    normed = x * inverse
-    grad_tokens = inverse * (dy - normed * jnp.mean(dy * normed, axis=-1, keepdims=True))
-    grad_tokens = jnp.where(jnp.repeat(live, block_rows)[:, None], grad_tokens, 0.0).astype(BF16)
+    got = []
+    for chunk in range(CHUNKS):
+        q = forward(chunk, source, xn, low, full_weight, up)
+        q = lax.all_to_all(q.reshape(blocks, block_rows, cols), DP, 0, 0, tiled=True)
+        got.append(jnp.take(q, pick, axis=0).reshape(capacity * block_rows, cols))
+    query = jnp.concatenate(got, axis=1)
+
+    grad_tokens = backward(
+        live.astype(jnp.int32), g, dlow, full_weight, full_down, tokens, gain_f.reshape(1, width), inverse
+    )
     return query, grad_tokens, grad_down, grad_up
 
 

time: 357 us -> 240 us (0.67)
  waiting for transfers between devices: 189 us -> 56.3 us
  Pallas kernels: 0 us -> 47.6 us
  matrix products: 58.4 us -> 11.1 us
  starting transfers between devices: 25.7 us -> 54.2 us
  blocking collectives: 27.8 us -> 0 us
  local copies, waits for them, and re-layouts: 21.6 us -> 33.7 us
    all_gather x1, waiting for transfers between devices: 81.2 us -> 0.01 us  [gather_weight(): both = lax.all_gather(piece, ('core', 'fsdp', 'x', 'y'), axis=0, tiled=True)]
    all_gather x1 -> x0, waiting for transfers between devices: 48.4 us -> none  [reduce_gradients(): return lax.all_gather(mine, DP, axis=0, tiled=True)]
    pallas_call x0 -> x3, Pallas kernels: none -> 47.6 us  [the longest x1 28.4 us: backward(): pl.pallas_call(backward_kernel, out_shape=jax.ShapeDtypeStruct((tokens, w...]
    dot_general x10 -> x4, matrix products: 58.4 us -> 11.1 us  [dot(): return lax.dot_general(a, b, (dims, ((), ())), preferred_element_type=F32)]
    psum x1 -> x0, waiting for transfers between devices: 35 us -> none  [reduce_gradients(): mine = lax.psum(mine, 'fsdp')]
    ppermute x3 -> x20, waiting for transfers between devices: 0.01 us -> 34.2 us  [fetch(): return lax.ppermute(v, axis, [((i + step) % n, i) for i in range(n)])]
    all_to_all x1 -> x0, blocking collectives: 27.8 us -> none  [reduce_gradients(): parts = lax.all_to_all(grads.astype(BF16), DP, 0, 0, tiled=True)]
    ppermute x3 -> x20, starting transfers between devices: 5.36 us -> 26.8 us  [fetch(): return lax.ppermute(v, axis, [((i + step) % n, i) for i in range(n)])]
  transfers between devices with their start and end apart: 9 -> 25, of which waited for: 5 -> 17; matrix products, arithmetic and copies ran while one was open for 16% -> 24% of each run, Pallas kernels for 0% -> 20%
where the time goes in v3:
time: 240 us; the launch traced here: 239 us
  waiting for transfers between devices  56.3 us (23%)
  starting transfers between devices  54.2 us (23%)
  Pallas kernels  47.6 us (20%)
  local copies, waits for them, and re-layouts  33.7 us (14%)
  other arithmetic  21.7 us (9%)
  between operations  14.5 us (6%)
  matrix products  11.1 us (5%)
    ppermute x20, waiting for transfers between devices, fetch(): return lax.ppermute(v, axis, [((i + step) % n, i) for i in range(n)])  34.2 us
    pallas_call x1, Pallas kernels, backward(): pl.pallas_call(backward_kernel, out_shape=jax.ShapeDtypeStruct((tokens, w...  28.4 us
    ppermute x20, starting transfers between devices, fetch(): return lax.ppermute(v, axis, [((i + step) % n, i) for i in range(n)])  26.8 us
    pallas_call x2, Pallas kernels, forward(): pl.pallas_call(forward_kernel, out_shape=jax.ShapeDtypeStruct((tokens, co...  19.2 us
    all_to_all x1, waiting for transfers between devices, body(): g_got = lax.all_to_all(g_send, DP, 0, 0, tiled=True)  16.2 us
    all_to_all x2, starting transfers between devices, body(): lax.all_to_all(q.reshape(blocks, block_rows, cols), DP, 0, 0, tiled=True)  14.4 us
    dot_general x4, matrix products, dot(): return lax.dot_general(a, b, (dims, ((), ())), preferred_element_type=F32)  11.1 us
    all_to_all x1, starting transfers between devices, body(): flags = lax.all_to_all(sent, DP, 0, 0, tiled=True)  8.6 us
  transfers between devices with their start and end apart: 25, of which 17 were waited for; matrix products, arithmetic and copies ran while one was open for 24% of the time, Pallas kernels for 20%

profile of v3, /device:TPU:1, one launch (start us, length us, event | category | flops | bytes accessed | tf_op | source)
XLA Modules:
  0.0 239.1 jit_solution(8348699376804744443)
XLA Ops:
  8.9 4.7 %collective-permute-start = (bf16[1152,128]{1,0:T(8,128)(2,1)}, bf16[1152,128]{1,0:T(8,128)(2,1)}, u32[]{:S(2)}, u32[]{:S(2)}) collective-permute-start(bf16[1152,128]{1,0:T(8,128)(2,1)} %param.13), channel_id=1, source_target_pairs={{1,0},{2,1},{3,2},{0,3},{5,4},{6,5},{7,6},{4,7},{9,8},{10,9},{11,1... | collective-permute-start | bytes 884744 | tf_op jit(solution)/shard_map/ppermute | solution.py:21
  17.0 8.6 %all-to-all-start.1 = ((s32[32,1,1]{2,1,0:T(1,128)}), s32[32,1,1]{2,1,0:T(1,128)S(1)}, u32[]{:S(2)}, u32[]{:S(2)}) async-start(s32[32,1,1]{2,1,0:T(1,128)} %copy.17), calls=%async_computation.1 | async-start | bytes 32768 | tf_op jit(solution)/shard_map/all_to_all | solution.py:194
  25.6 3.3 %fusion = f32[512]{0:T(512)S(1)} fusion(bf16[512,4608]{1,0:T(8,128)(2,1)} %x.1), kind=kLoop, calls=%fused_computation.6 | loop fusion | flops 7077376 | bytes 4720640 | tf_op jit(solution)/shard_map/reduce_sum | solution.py:210
  29.0 3.5 %all-to-all-done.1 = s32[32,1,1]{2,1,0:T(1,128)S(1)} async-done(((s32[32,1,1]{2,1,0:T(1,128)}), s32[32,1,1]{2,1,0:T(1,128)S(1)}, u32[]{:S(2)}, u32[]{:S(2)}) %all-to-all-start.1) | async-done | bytes 160 | tf_op jit(solution)/shard_map/all_to_all | solution.py:194
  36.0 4.3 %all-to-all-start.3 = ((bf16[32,16,2048]{2,1,0:T(8,128)(2,1)}), bf16[32,16,2048]{2,1,0:T(8,128)(2,1)S(1)}, u32[]{:S(2)}, u32[]{:S(2)}) async-start(bf16[32,16,2048]{2,1,0:T(8,128)(2,1)} %broadcast_select_fusion), calls=%async_computation.3 | async-start | bytes 4194304 | tf_op jit(solution)/shard_map/all_to_all | solution.py:205
  40.4 6.1 %fusion.2.xn = bf16[512,4608]{1,0:T(8,128)(2,1)} fusion(bf16[512,4608]{1,0:T(8,128)(2,1)} %x.1, f32[4608]{0:T(1024)S(1)} %convert_element_type.56, f32[512]{0:T(512)S(1)} %add_rsqrt_fusion), kind=kLoop, calls=%fused_computation.8 | loop fusion | flops 9437184 | bytes 9457664 | tf_op jit(solution)/shard_map/convert_element_type | solution.py:212
  52.9 4.1 %fusion.14.low = bf16[512,128]{1,0:T(8,128)(2,1)S(1)} fusion(bf16[512,4608]{1,0:T(8,128)(2,1)} %fusion.2.xn, bf16[4608,128]{1,0:T(8,128)(2,1)} %constant_dynamic-update-slice_fusion.10.down), kind=kOutput, calls=%fused_computation.77 | convolution fusion | flops 603979776 | bytes 6029312 | tf_op jit(solution)/shard_map/dot_general | solution.py:16
  57.0 16.2 %all-to-all-done.3 = bf16[32,16,2048]{2,1,0:T(8,128)(2,1)S(1)} async-done(((bf16[32,16,2048]{2,1,0:T(8,128)(2,1)}), bf16[32,16,2048]{2,1,0:T(8,128)(2,1)S(1)}, u32[]{:S(2)}, u32[]{:S(2)}) %all-to-all-start.3) | async-done | bytes 2097184 | tf_op jit(solution)/shard_map/all_to_all | solution.py:205
  78.6 2.4 reshape.122
  81.7 4.8 %fusion.15 = f32[4608,128]{1,0:T(8,128)S(1)} fusion(bf16[512,4608]{1,0:T(8,128)(2,1)} %fusion.2.xn, bf16[512,128]{1,0:T(8,128)(2,1)S(1)} %convolution_convert_fusion.dlow), kind=kOutput, calls=%fused_computation.78 | convolution fusion | flops 603979776 | bytes 7208960 | tf_op jit(solution)/shard_map/dot_general | solution.py:16
  99.5 8.6 %collective-permute-done.6 = bf16[832,128]{1,0:T(8,128)(2,1)S(1)} collective-permute-done((bf16[832,128]{1,0:T(8,128)(2,1)S(1)}, bf16[832,128]{1,0:T(8,128)(2,1)S(1)}, u32[]{:S(2)}, u32[]{:S(2)}) %collective-permute-start.6) | collective-permute-done | bytes 213024 | tf_op jit(solution)/shard_map/ppermute | solution.py:21
  108.1 9.5 %collective-permute-done.5 = bf16[832,128]{1,0:T(8,128)(2,1)S(1)} collective-permute-done((bf16[832,128]{1,0:T(8,128)(2,1)S(1)}, bf16[832,128]{1,0:T(8,128)(2,1)S(1)}, u32[]{:S(2)}, u32[]{:S(2)}) %collective-permute-start.5) | collective-permute-done | bytes 213024 | tf_op jit(solution)/shard_map/ppermute | solution.py:21
  125.3 2.4 %collective-permute-start.10 = (f32[208,128]{1,0:T(8,128)S(1)}, f32[208,128]{1,0:T(8,128)S(1)}, u32[]{:S(2)}, u32[]{:S(2)}) collective-permute-start(f32[208,128]{1,0:T(8,128)S(1)} %get-tuple-element.6), channel_id=1, source_target_pairs={{8,0},{16,8},{24,16},{0,24},{9,1},{17,9},{25,17},{1,25},{10,2},{18... | collective-permute-start | bytes 319496 | tf_op jit(solution)/shard_map/ppermute | solution.py:21
  129.5 3.3 %collective-permute-done.11 = f32[208,128]{1,0:T(8,128)S(1)} collective-permute-done((f32[208,128]{1,0:T(8,128)S(1)}, f32[208,128]{1,0:T(8,128)S(1)}, u32[]{:S(2)}, u32[]{:S(2)}) %collective-permute-start.11) | collective-permute-done | bytes 106528 | tf_op jit(solution)/shard_map/ppermute | solution.py:21
  134.0 4.1 %collective-permute-start.13 = (bf16[208,128]{1,0:T(8,128)(2,1)S(1)}, bf16[208,128]{1,0:T(8,128)(2,1)S(1)}, u32[]{:S(2)}, u32[]{:S(2)}) collective-permute-start(bf16[208,128]{1,0:T(8,128)(2,1)S(1)} %reduce_sum.49), channel_id=1, source_target_pairs={{32,0},{64,32},{96,64},{0,96},{33,1},{65,33},{97,65},{1,97},{34,2}... | collective-permute-start | bytes 159752 | tf_op jit(solution)/shard_map/ppermute | solution.py:21
  139.3 3.4 %collective-permute-done.14 = bf16[208,128]{1,0:T(8,128)(2,1)S(1)} collective-permute-done((bf16[208,128]{1,0:T(8,128)(2,1)S(1)}, bf16[208,128]{1,0:T(8,128)(2,1)S(1)}, u32[]{:S(2)}, u32[]{:S(2)}) %collective-permute-start.14) | collective-permute-done | bytes 53280 | tf_op jit(solution)/shard_map/ppermute | solution.py:21
  151.5 2.3 copy-done.2
  153.9 9.6 %forward.2 = bf16[512,1024]{1,0:T(8,128)(2,1)} custom-call(s32[32]{0:T(128)S(1)} %select_reduce_fusion.1.source, bf16[512,4608]{1,0:T(8,128)(2,1)S(1)} %copy-done.2, bf16[512,128]{1,0:T(8,128)(2,1)S(1)} %fusion.14.low, bf16[2,4608,1024]{2,1,0:T(8,128)(2,1)} %bitcast.34, bf16[128,2048]{1,0:T(8,128)(2,1)S(1)} %copy-done.4), custom_call_target="tpu_custom_call" | custom-call | flops 4831838208 | bytes 16777216 | tf_op jit(solution)/shard_map/forward/pallas_call | solution.py:101
  163.4 9.6 %all-to-all-start = ((bf16[32,16,1024]{2,1,0:T(8,128)(2,1)}), bf16[32,16,1024]{2,1,0:T(8,128)(2,1)}, u32[]{:S(2)}, u32[]{:S(2)}) async-start(bf16[32,16,1024]{2,1,0:T(8,128)(2,1)} %bitcast.2), calls=%async_computation | async-start | bytes 2097152 | tf_op jit(solution)/shard_map/all_to_all | solution.py:224
  175.6 2.3 copy-done.3
  177.9 9.6 %forward.3 = bf16[512,1024]{1,0:T(8,128)(2,1)} custom-call(s32[32]{0:T(128)S(1)} %select_reduce_fusion.1.source, bf16[512,4608]{1,0:T(8,128)(2,1)S(1)} %copy-done.3, bf16[512,128]{1,0:T(8,128)(2,1)S(1)} %fusion.14.low, bf16[2,4608,1024]{2,1,0:T(8,128)(2,1)} %bitcast.35, bf16[128,2048]{1,0:T(8,128)(2,1)S(1)} %copy-done.4), custom_call_target="tpu_custom_call" | custom-call | flops 4831838208 | bytes 16777216 | tf_op jit(solution)/shard_map/forward/pallas_call | solution.py:101
  187.5 2.5 %all-to-all-done = bf16[32,16,1024]{2,1,0:T(8,128)(2,1)} async-done(((bf16[32,16,1024]{2,1,0:T(8,128)(2,1)}), bf16[32,16,1024]{2,1,0:T(8,128)(2,1)}, u32[]{:S(2)}, u32[]{:S(2)}) %all-to-all-start) | async-done | bytes 1048608 | tf_op jit(solution)/shard_map/all_to_all | solution.py:224
  190.0 4.8 %all-to-all-start.2 = ((bf16[32,16,1024]{2,1,0:T(8,128)(2,1)}), bf16[32,16,1024]{2,1,0:T(8,128)(2,1)}, u32[]{:S(2)}, u32[]{:S(2)}) async-start(bf16[32,16,1024]{2,1,0:T(8,128)(2,1)} %bitcast.4), calls=%async_computation.2 | async-start | bytes 2097152 | tf_op jit(solution)/shard_map/all_to_all | solution.py:224
  198.9 28.4 %backward.1 = bf16[512,4608]{1,0:T(8,128)(2,1)} custom-call(s32[32]{0:T(128)} %get-tuple-element.15.live, bf16[512,2048]{1,0:T(8,128)(2,1)} %copy-done.5, bf16[512,128]{1,0:T(8,128)(2,1)} %copy-done.7, bf16[2,4608,1024]{2,1,0:T(8,128)(2,1)} %bitcast.36, bf16[4608,128]{1,0:T(8,128)(2,1)} %constant_dynamic-update-slice_fusion.10.down, bf16[512,4608]{1,0:T(8,128)(2,1)} %x.1, ...), custom_call_target="tpu_custom_call" | custom-call | flops 9663676416 | bytes 33554432 | tf_op jit(solution)/shard_map/backward/pallas_call | solution.py:154
  (141 shorter events, 66.1 us)
Async XLA Ops:
  7.2 144.3 %all-gather.2.cloned.1.call-start = ((), (), s32[]{:S(2)}) async-start(), calls=%async_computation.4 | async-start | bytes 19021824 | tf_op jit(solution)/shard_map/all_gather | solution.py:39
  8.9 39.8 %collective-permute-start = (bf16[1152,128]{1,0:T(8,128)(2,1)}, bf16[1152,128]{1,0:T(8,128)(2,1)}, u32[]{:S(2)}, u32[]{:S(2)}) collective-permute-start(bf16[1152,128]{1,0:T(8,128)(2,1)} %param.13), channel_id=1, source_target_pairs={{1,0},{2,1},{3,2},{0,3},{5,4},{6,5},{7,6},{4,7},{9,8},{10,9},{11,1... | collective-permute-start | bytes 884744 | tf_op jit(solution)/shard_map/ppermute | solution.py:21
  13.6 36.9 %collective-permute-start.1 = (bf16[1152,128]{1,0:T(8,128)(2,1)}, bf16[1152,128]{1,0:T(8,128)(2,1)}, u32[]{:S(2)}, u32[]{:S(2)}) collective-permute-start(bf16[1152,128]{1,0:T(8,128)(2,1)} %param.13), channel_id=1, source_target_pairs={{2,0},{3,1},{0,2},{1,3},{6,4},{7,5},{4,6},{5,7},{10,8},{11,9},{8,1... | collective-permute-start | bytes 884744 | tf_op jit(solution)/shard_map/ppermute | solution.py:21
  13.6 38.6 %collective-permute-start.2 = (bf16[1152,128]{1,0:T(8,128)(2,1)}, bf16[1152,128]{1,0:T(8,128)(2,1)S(1)}, u32[]{:S(2)}, u32[]{:S(2)}) collective-permute-start(bf16[1152,128]{1,0:T(8,128)(2,1)} %param.13), channel_id=1, source_target_pairs={{3,0},{0,1},{1,2},{2,3},{7,4},{4,5},{5,6},{6,7},{11,8},{8,9},{9,10... | collective-permute-start | bytes 884744 | tf_op jit(solution)/shard_map/ppermute | solution.py:21
  17.0 15.5 %all-to-all-start.1 = ((s32[32,1,1]{2,1,0:T(1,128)}), s32[32,1,1]{2,1,0:T(1,128)S(1)}, u32[]{:S(2)}, u32[]{:S(2)}) async-start(s32[32,1,1]{2,1,0:T(1,128)} %copy.17), calls=%async_computation.1 | async-start | bytes 32768 | tf_op jit(solution)/shard_map/all_to_all | solution.py:194
  36.0 37.2 %all-to-all-start.3 = ((bf16[32,16,2048]{2,1,0:T(8,128)(2,1)}), bf16[32,16,2048]{2,1,0:T(8,128)(2,1)S(1)}, u32[]{:S(2)}, u32[]{:S(2)}) async-start(bf16[32,16,2048]{2,1,0:T(8,128)(2,1)} %broadcast_select_fusion), calls=%async_computation.3 | async-start | bytes 4194304 | tf_op jit(solution)/shard_map/all_to_all | solution.py:205
  95.1 13.0 %collective-permute-start.6 = (bf16[832,128]{1,0:T(8,128)(2,1)S(1)}, bf16[832,128]{1,0:T(8,128)(2,1)S(1)}, u32[]{:S(2)}, u32[]{:S(2)}) collective-permute-start(bf16[832,128]{1,0:T(8,128)(2,1)S(1)} %get-tuple-element.10), channel_id=1, source_target_pairs={{3,0},{0,1},{1,2},{2,3},{7,4},{4,5},{5,6},{6,7},{11,8},{8,9},{9,10... | collective-permute-start | bytes 638984 | tf_op jit(solution)/shard_map/ppermute | solution.py:21
  96.5 21.1 %collective-permute-start.5 = (bf16[832,128]{1,0:T(8,128)(2,1)S(1)}, bf16[832,128]{1,0:T(8,128)(2,1)S(1)}, u32[]{:S(2)}, u32[]{:S(2)}) collective-permute-start(bf16[832,128]{1,0:T(8,128)(2,1)S(1)} %get-tuple-element.11), channel_id=1, source_target_pairs={{2,0},{3,1},{0,2},{1,3},{6,4},{7,5},{4,6},{5,7},{10,8},{11,9},{8,1... | collective-permute-start | bytes 638984 | tf_op jit(solution)/shard_map/ppermute | solution.py:21
  98.3 19.5 %collective-permute-start.4 = (bf16[832,128]{1,0:T(8,128)(2,1)S(1)}, bf16[832,128]{1,0:T(8,128)(2,1)S(1)}, u32[]{:S(2)}, u32[]{:S(2)}) collective-permute-start(bf16[832,128]{1,0:T(8,128)(2,1)S(1)} %get-tuple-element.9), channel_id=1, source_target_pairs={{1,0},{2,1},{3,2},{0,3},{5,4},{6,5},{7,6},{4,7},{9,8},{10,9},{11,1... | collective-permute-start | bytes 638984 | tf_op jit(solution)/shard_map/ppermute | solution.py:21
  117.9 4.9 %collective-permute-start.9 = (f32[208,128]{1,0:T(8,128)S(1)}, f32[208,128]{1,0:T(8,128)S(1)}, u32[]{:S(2)}, u32[]{:S(2)}) collective-permute-start(f32[208,128]{1,0:T(8,128)S(1)} %get-tuple-element.13), channel_id=1, source_target_pairs={{96,0},{0,32},{32,64},{64,96},{97,1},{1,33},{33,65},{65,97},{98,2}... | collective-permute-start | bytes 319496 | tf_op jit(solution)/shard_map/ppermute | solution.py:21
  118.7 5.3 %collective-permute-start.8 = (f32[208,128]{1,0:T(8,128)S(1)}, f32[208,128]{1,0:T(8,128)S(1)}, u32[]{:S(2)}, u32[]{:S(2)}) collective-permute-start(f32[208,128]{1,0:T(8,128)S(1)} %get-tuple-element.14), channel_id=1, source_target_pairs={{64,0},{96,32},{0,64},{32,96},{65,1},{97,33},{1,65},{33,97},{66,2}... | collective-permute-start | bytes 319496 | tf_op jit(solution)/shard_map/ppermute | solution.py:21
  119.5 5.7 %collective-permute-start.7 = (f32[208,128]{1,0:T(8,128)S(1)}, f32[208,128]{1,0:T(8,128)S(1)}, u32[]{:S(2)}, u32[]{:S(2)}) collective-permute-start(f32[208,128]{1,0:T(8,128)S(1)} %get-tuple-element.12), channel_id=1, source_target_pairs={{32,0},{64,32},{96,64},{0,96},{33,1},{65,33},{97,65},{1,97},{34,2}... | collective-permute-start | bytes 319496 | tf_op jit(solution)/shard_map/ppermute | solution.py:21
  125.3 4.2 %collective-permute-start.10 = (f32[208,128]{1,0:T(8,128)S(1)}, f32[208,128]{1,0:T(8,128)S(1)}, u32[]{:S(2)}, u32[]{:S(2)}) collective-permute-start(f32[208,128]{1,0:T(8,128)S(1)} %get-tuple-element.6), channel_id=1, source_target_pairs={{8,0},{16,8},{24,16},{0,24},{9,1},{17,9},{25,17},{1,25},{10,2},{18... | collective-permute-start | bytes 319496 | tf_op jit(solution)/shard_map/ppermute | solution.py:21
  127.8 5.1 %collective-permute-start.11 = (f32[208,128]{1,0:T(8,128)S(1)}, f32[208,128]{1,0:T(8,128)S(1)}, u32[]{:S(2)}, u32[]{:S(2)}) collective-permute-start(f32[208,128]{1,0:T(8,128)S(1)} %get-tuple-element.6), channel_id=1, source_target_pairs={{16,0},{24,8},{0,16},{8,24},{17,1},{25,9},{1,17},{9,25},{18,2},{26... | collective-permute-start | bytes 319496 | tf_op jit(solution)/shard_map/ppermute | solution.py:21
  129.1 4.9 %collective-permute-start.12 = (f32[208,128]{1,0:T(8,128)S(1)}, f32[208,128]{1,0:T(8,128)S(1)}, u32[]{:S(2)}, u32[]{:S(2)}) collective-permute-start(f32[208,128]{1,0:T(8,128)S(1)} %get-tuple-element.6), channel_id=1, source_target_pairs={{24,0},{0,8},{8,16},{16,24},{25,1},{1,9},{9,17},{17,25},{26,2},{2,... | collective-permute-start | bytes 319496 | tf_op jit(solution)/shard_map/ppermute | solution.py:21
  134.0 5.3 %collective-permute-start.13 = (bf16[208,128]{1,0:T(8,128)(2,1)S(1)}, bf16[208,128]{1,0:T(8,128)(2,1)S(1)}, u32[]{:S(2)}, u32[]{:S(2)}) collective-permute-start(bf16[208,128]{1,0:T(8,128)(2,1)S(1)} %reduce_sum.49), channel_id=1, source_target_pairs={{32,0},{64,32},{96,64},{0,96},{33,1},{65,33},{97,65},{1,97},{34,2}... | collective-permute-start | bytes 159752 | tf_op jit(solution)/shard_map/ppermute | solution.py:21
  138.1 4.6 %collective-permute-start.14 = (bf16[208,128]{1,0:T(8,128)(2,1)S(1)}, bf16[208,128]{1,0:T(8,128)(2,1)S(1)}, u32[]{:S(2)}, u32[]{:S(2)}) collective-permute-start(bf16[208,128]{1,0:T(8,128)(2,1)S(1)} %reduce_sum.49), channel_id=1, source_target_pairs={{64,0},{96,32},{0,64},{32,96},{65,1},{97,33},{1,65},{33,97},{66,2}... | collective-permute-start | bytes 159752 | tf_op jit(solution)/shard_map/ppermute | solution.py:21
  138.1 4.8 %collective-permute-start.15 = (bf16[208,128]{1,0:T(8,128)(2,1)S(1)}, bf16[208,128]{1,0:T(8,128)(2,1)S(1)}, u32[]{:S(2)}, u32[]{:S(2)}) collective-permute-start(bf16[208,128]{1,0:T(8,128)(2,1)S(1)} %reduce_sum.49), channel_id=1, source_target_pairs={{96,0},{0,32},{32,64},{64,96},{97,1},{1,33},{33,65},{65,97},{98,2}... | collective-permute-start | bytes 159752 | tf_op jit(solution)/shard_map/ppermute | solution.py:21
  142.9 6.0 %collective-permute-start.16 = (bf16[832,128]{1,0:T(8,128)(2,1)S(1)}, bf16[832,128]{1,0:T(8,128)(2,1)S(1)}, u32[]{:S(2)}, u32[]{:S(2)}) collective-permute-start(bf16[832,128]{1,0:T(8,128)(2,1)S(1)} %constant_dynamic-update-slice_fusion.6), channel_id=1, source_target_pairs={{1,0},{2,1},{3,2},{0,3},{5,4},{6,5},{7,6},{4,7},{9,8},{10,9},{11,1... | collective-permute-start | bytes 638984 | tf_op jit(solution)/shard_map/ppermute | solution.py:21
  144.5 6.3 %collective-permute-start.17 = (bf16[832,128]{1,0:T(8,128)(2,1)S(1)}, bf16[832,128]{1,0:T(8,128)(2,1)S(1)}, u32[]{:S(2)}, u32[]{:S(2)}) collective-permute-start(bf16[832,128]{1,0:T(8,128)(2,1)S(1)} %constant_dynamic-update-slice_fusion.6), channel_id=1, source_target_pairs={{2,0},{3,1},{0,2},{1,3},{6,4},{7,5},{4,6},{5,7},{10,8},{11,9},{8,1... | collective-permute-start | bytes 638984 | tf_op jit(solution)/shard_map/ppermute | solution.py:21
  146.4 26.6 %collective-permute-start.18 = (bf16[832,128]{1,0:T(8,128)(2,1)S(1)}, bf16[832,128]{1,0:T(8,128)(2,1)S(1)}, u32[]{:S(2)}, u32[]{:S(2)}) collective-permute-start(bf16[832,128]{1,0:T(8,128)(2,1)S(1)} %constant_dynamic-update-slice_fusion.6), channel_id=1, source_target_pairs={{3,0},{0,1},{1,2},{2,3},{7,4},{4,5},{5,6},{6,7},{11,8},{8,9},{9,10... | collective-permute-start | bytes 638984 | tf_op jit(solution)/shard_map/ppermute | solution.py:21
  163.4 26.6 %all-to-all-start = ((bf16[32,16,1024]{2,1,0:T(8,128)(2,1)}), bf16[32,16,1024]{2,1,0:T(8,128)(2,1)}, u32[]{:S(2)}, u32[]{:S(2)}) async-start(bf16[32,16,1024]{2,1,0:T(8,128)(2,1)} %bitcast.2), calls=%async_computation | async-start | bytes 2097152 | tf_op jit(solution)/shard_map/all_to_all | solution.py:224
  173.7 21.1 %collective-permute-start.19 = (bf16[3328,128]{1,0:T(8,128)(2,1)}, bf16[3328,128]{1,0:T(8,128)(2,1)}, u32[]{:S(2)}, u32[]{:S(2)}) collective-permute-start(bf16[3328,128]{1,0:T(8,128)(2,1)} %constant_dynamic-update-slice_fusion.2), channel_id=1, source_target_pairs={{4,0},{0,4},{5,1},{1,5},{6,2},{2,6},{7,3},{3,7},{12,8},{8,12},{13,... | collective-permute-start | bytes 2555912 | tf_op jit(solution)/shard_map/ppermute | solution.py:21
  190.0 39.1 %all-to-all-start.2 = ((bf16[32,16,1024]{2,1,0:T(8,128)(2,1)}), bf16[32,16,1024]{2,1,0:T(8,128)(2,1)}, u32[]{:S(2)}, u32[]{:S(2)}) async-start(bf16[32,16,1024]{2,1,0:T(8,128)(2,1)} %bitcast.4), calls=%async_computation.2 | async-start | bytes 2097152 | tf_op jit(solution)/shard_map/all_to_all | solution.py:224
  (20 other events, 125.6 us)
Sparse Core Ops, SparseCore 0:
  11.0 111.1 all-gather.1

commit v4 on v3

v4 whole, which is shorter than its diff:
```python
import jax
import jax.numpy as jnp
from jax import lax
from jax.experimental import pallas as pl
from jax.experimental.pallas import tpu as pltpu
from jax.sharding import Mesh, PartitionSpec as P

DP = ("x", "y", "core")
BF16 = jnp.bfloat16
F32 = jnp.float32
MIB = 1024 * 1024


def dot(a, b, dims=((1,), (0,))):
    return lax.dot_general(a, b, (dims, ((), ())), preferred_element_type=F32)


def fetch(v, axis, step):
    n = lax.axis_size(axis)
    return lax.ppermute(v, axis, [((i + step) % n, i) for i in range(n)])


def gather_down(down):
    me = lax.axis_index("fsdp")
    rows = down.shape[0]
    full = jnp.zeros((4 * rows, down.shape[1]), down.dtype)
    for step in range(4):
        part = fetch(down, "fsdp", step) if step else down
        full = lax.dynamic_update_slice(full, part, (((me + step) % 4) * rows, 0))
    return full


def gather_weight(weight):
    chip = lax.axis_index("x") * 4 + lax.axis_index("y")
    half = weight.shape[1] // 2
    rows = weight.shape[0] // 16
    piece = lax.dynamic_slice(weight, (chip * rows, lax.axis_index("core") * half), (rows, half))
    both = lax.all_gather(piece, ("core", "fsdp", "x", "y"), axis=0, tiled=True)
    return both.reshape(2, both.shape[0] // 2, half)


def sum_scatter(v, axis, wire):
    n = lax.axis_size(axis)
    me = lax.axis_index(axis)
    m = v.shape[0] // n
    total = lax.dynamic_slice_in_dim(v, me * m, m, 0)
    for step in range(1, n):
        part = lax.dynamic_slice_in_dim(v, ((me + n - step) % n) * m, m, 0).astype(wire)
        total = total + fetch(part, axis, step).astype(F32)
    return total


def sum_all(v, axis):
    n = lax.axis_size(axis)
    me = lax.axis_index(axis)
    parts = jnp.zeros((n,) + v.shape, v.dtype)
    for step in range(n):
        part = fetch(v, axis, step) if step else v
        parts = lax.dynamic_update_slice(parts, part[None], ((me + step) % n, 0, 0))
    return jnp.sum(parts, axis=0)


def tie(value, *others):
    return lax.optimization_barrier((value,) + others)[0]


def forward_kernel(source, xn, low, w, up, out, q):
    q[...] = (dot(xn[...], w[0]) + dot(low[...], up[...])).astype(BF16)

    def place(d, carry):
        row = pl.multiple_of(source[d] * 16, 16)
        out[pl.ds(pl.multiple_of(d * 16, 16), 16), :] = q[pl.ds(row, 16), :]
        return carry

    lax.fori_loop(0, out.shape[0] // 16, place, 0)


def forward(source, xn, low, w, up):
    tokens, width = xn.shape
    tile = 512
    per_half = w.shape[2] // tile
    cols = 2 * w.shape[2]
    return pl.pallas_call(
        forward_kernel,
        out_shape=jax.ShapeDtypeStruct((tokens, cols), BF16),
        grid_spec=pltpu.PrefetchScalarGridSpec(
            num_scalar_prefetch=1,
            grid=(cols // tile,),
            in_specs=[
                pl.BlockSpec((tokens, width), lambda i, s: (0, 0)),
                pl.BlockSpec(low.shape, lambda i, s: (0, 0)),
                pl.BlockSpec((1, width, tile), lambda i, s: (i // per_half, 0, i % per_half)),
                pl.BlockSpec((up.shape[0], tile), lambda i, s: (0, i)),
            ],
            out_specs=pl.BlockSpec((tokens, tile), lambda i, s: (0, i)),
            scratch_shapes=[pltpu.VMEM((tokens, tile), BF16)],
        ),
        compiler_params=pltpu.CompilerParams(vmem_limit_bytes=40 * MIB),
        cost_estimate=pl.CostEstimate(
            flops=2 * tokens * width * cols, bytes_accessed=26 * MIB, transcendentals=0
        ),
        name="forward",
    )(source, xn, low, w, up)


def backward_kernel(live, g, dlow, w, down, x, gain, inverse, out, held_dy, held_x, stat):
    i = pl.program_id(0)
    n = pl.num_programs(0)
    nt = ((1,), (1,))
    half = w.shape[2]
    tile = w.shape[1]
    inv = inverse[...]
    acc = dot(g[:, :half], w[0], nt) + dot(g[:, half:], w[1], nt) + dot(dlow[...], down[...], nt)
    dy = acc * gain[...]
    part = jnp.sum(dy * x[...].astype(F32), axis=-1, keepdims=True)
    stat[...] = part + jnp.where(i == 0, 0.0, stat[...])
    held_dy[i] = dy
    held_x[i] = x[...]

    @pl.when(i == n - 1)
    def _():
        factor = stat[...] * inv * inv * inv * (1.0 / (n * tile))
        stat[...] = factor

        def finish(j, carry):
            r = pl.ds(pl.multiple_of(j * 16, 16), 16)
            keep = live[j] > 0
            scale = inverse[r, :]
            shift = stat[r, :]
            for t in range(width_tiles(out, tile)):
                res = scale * held_dy[t, r, :] - shift * held_x[t, r, :].astype(F32)
                out[r, t * tile : (t + 1) * tile] = jnp.where(keep, res, 0.0).astype(BF16)
            return carry

        lax.fori_loop(0, out.shape[0] // 16, finish, 0)


def width_tiles(out, tile):
    return out.shape[1] // tile


def backward(live, g, dlow, w, down, x, gain, inverse):
    tokens, width = x.shape
    tile = 512
    n = width // tile
    cols = 2 * w.shape[2]
    return pl.pallas_call(
        backward_kernel,
        out_shape=jax.ShapeDtypeStruct((tokens, width), BF16),
        grid_spec=pltpu.PrefetchScalarGridSpec(
            num_scalar_prefetch=1,
            grid=(n,),
            in_specs=[
                pl.BlockSpec((tokens, cols), lambda i, s: (0, 0)),
                pl.BlockSpec(dlow.shape, lambda i, s: (0, 0)),
                pl.BlockSpec((2, tile, cols // 2), lambda i, s: (0, i, 0)),
                pl.BlockSpec((tile, down.shape[1]), lambda i, s: (i, 0)),
                pl.BlockSpec((tokens, tile), lambda i, s: (0, i)),
                pl.BlockSpec((1, tile), lambda i, s: (0, i)),
                pl.BlockSpec((tokens, 1), lambda i, s: (0, 0)),
            ],
            out_specs=pl.BlockSpec((tokens, width), lambda i, s: (0, 0)),
            scratch_shapes=[
                pltpu.VMEM((n, tokens, tile), F32),
                pltpu.VMEM((n, tokens, tile), BF16),
                pltpu.VMEM((tokens, 1), F32),
            ],
        ),
        compiler_params=pltpu.CompilerParams(vmem_limit_bytes=48 * MIB),
        cost_estimate=pl.CostEstimate(
            flops=2 * tokens * width * cols, bytes_accessed=32 * MIB, transcendentals=0
        ),
        name="backward",
    )(live, g, dlow, w, down, x, gain, inverse)


def body(tokens, gain, weight, down, up, depth, destination, cotangent):
    blocks = depth.shape[0]
    rows, width = tokens.shape
    block_rows = rows // blocks
    features = cotangent.shape[1]
    capacity = cotangent.shape[0] // block_rows
    live = depth >= 2
    dest = jnp.clip(destination, 0, 31)

    hit = live[None, :] & (dest[None, :] == jnp.arange(32, dtype=jnp.int32)[:, None])
    order = jnp.arange(blocks, dtype=jnp.int32)
    source = jnp.sum(jnp.where(hit, order[None, :], 0), axis=1)
    sent = jnp.any(hit, axis=1).astype(jnp.int32)
    flags = lax.all_to_all(sent, DP, 0, 0, tiled=True)
    rank = jnp.sum(jnp.where(order[None, :] < order[:, None], flags[None, :], 0), axis=1)
    seat = jnp.clip(rank, 0, capacity - 1)
    seats = jnp.arange(capacity, dtype=jnp.int32)
    match = (flags[None, :] > 0) & (rank[None, :] == seats[:, None])
    pick = jnp.sum(jnp.where(match, order[None, :], 0), axis=1)

    full_down = gather_down(down)
    x = tokens.astype(F32)
    inverse = lax.rsqrt(jnp.mean(x * x, axis=-1, keepdims=True) + 1e-06)
    weight, down = lax.optimization_barrier((weight, down, inverse))[:2]
    full_weight = gather_weight(weight)
    full_down = gather_down(down)
    gain_f = gain.astype(F32)
    xn = (x * inverse * gain_f).astype(BF16)
    low = dot(xn, full_down).astype(BF16)

    rank_width = low.shape[1]
    dlow_own = dot(cotangent, up, ((1,), (1,))).astype(BF16)
    narrow = jnp.concatenate(
        [
            jnp.take(low.reshape(blocks, block_rows, rank_width), source, axis=0),
            jnp.take(dlow_own.reshape(capacity, block_rows, rank_width), seat, axis=0),
        ],
        axis=2,
    )
    narrow = lax.all_to_all(narrow, DP, 0, 0, tiled=True)
    low_own = jnp.take(narrow[:, :, :rank_width], pick, axis=0).reshape(-1, rank_width)
    dlow = jnp.take(narrow[:, :, rank_width:], dest, axis=0)
    dlow = jnp.where(live[:, None, None], dlow, jnp.zeros((), BF16)).reshape(rows, rank_width)

    g_send = jnp.take(cotangent.reshape(capacity, block_rows, features), seat, axis=0)
    g_send = tie(g_send, narrow)
    g_got = lax.all_to_all(g_send, DP, 0, 0, tiled=True)
    g = jnp.where(live[:, None, None], jnp.take(g_got, dest, axis=0), jnp.zeros((), BF16))
    g = g.reshape(rows, features)

    grad_up = dot(low_own, cotangent, ((0,), (0,)))
    grad_down = dot(xn, dlow, ((0,), (0,)))
    lanes = features // rank_width
    grad_up = jnp.swapaxes(grad_up.reshape(rank_width, lanes, rank_width), 0, 1)
    grads = jnp.concatenate([grad_down, grad_up.reshape(features, rank_width)], axis=0)
    share = sum_scatter(grads, "core", F32)
    share = tie(sum_scatter(share, "fsdp", BF16), g_got)
    share = sum_scatter(share, "x", F32)
    share = sum_all(share, "y").astype(BF16)
    full_weight, share = lax.optimization_barrier((full_weight, share))
    grads = lax.all_gather(share, ("core", "fsdp", "x"), axis=0, tiled=True).astype(F32)
    grad_down = grads[:width]
    grad_up = jnp.swapaxes(grads[width:].reshape(lanes, rank_width, rank_width), 0, 1)
    grad_up = grad_up.reshape(rank_width, features)

    q = forward(source, xn, low, full_weight, up).reshape(blocks, block_rows, features)
    q = lax.all_to_all(q, DP, 0, 0, tiled=True)
    query = jnp.take(q, pick, axis=0).reshape(capacity * block_rows, features)

    grad_tokens = backward(
        live.astype(jnp.int32), g, dlow, full_weight, full_down, tokens, gain_f.reshape(1, width), inverse
    )
    return query, grad_tokens, grad_down, grad_up


def solution(mesh):
    fine = Mesh(mesh.devices.reshape(4, 4, 2, 4), ("x", "y", "core", "fsdp"))
    split = P(("x", "y", "core", "fsdp"))
    in_specs = (split, P(), P("fsdp"), P("fsdp"), P(), split, split, split)
    return jax.shard_map(
        body, mesh=fine, in_specs=in_specs, out_specs=(split, split, P(), P()), check_vma=False
    )
```

time: 240 us -> 214 us (0.89)
  starting transfers between devices: 54.2 us -> 42.4 us
  Pallas kernels: 47.6 us -> 38.4 us
  local copies, waits for them, and re-layouts: 33.7 us -> 26 us
  other arithmetic: 21.7 us -> 24.2 us
    ppermute x20 -> x13, starting transfers between devices: 26.8 us -> 14.8 us  [fetch(): return lax.ppermute(v, axis, [((i + step) % n, i) for i in range(n)])]
    all_to_all x2, waiting for transfers between devices: 2.48 us -> 13.8 us  [the longest x1 11 us: body(): narrow = lax.all_to_all(narrow, DP, 0, 0, tiled=True)]
    pallas_call x1, Pallas kernels: 28.4 us -> 22.8 us  [backward(): pl.pallas_call(backward_kernel, out_shape=jax.ShapeDtypeStruct((tokens, w...]
    dynamic_update_slice x10 -> x0, local copies, waits for them, and re-layouts: 5.39 us -> none  [collect(): full = lax.dynamic_update_slice(full, part, ((me + step) % n * m, 0))]
    ppermute x20 -> x13, waiting for transfers between devices: 34.2 us -> 29.2 us  [fetch(): return lax.ppermute(v, axis, [((i + step) % n, i) for i in range(n)])]
    pallas_call x2 -> x1, Pallas kernels: 19.2 us -> 15.6 us  [forward(): pl.pallas_call(forward_kernel, out_shape=jax.ShapeDtypeStruct((tokens, co...]
    all_to_all x1, waiting for transfers between devices: 3.49 us -> 0.01 us  [body(): flags = lax.all_to_all(sent, DP, 0, 0, tiled=True)]
    reshape x2 -> x1, local copies, waits for them, and re-layouts: 3.48 us -> 0.61 us  [body(): grads[width:].reshape(lanes, rank_width, rank_width)]
  transfers between devices with their start and end apart: 25 -> 19, of which waited for: 17 -> 12; matrix products, arithmetic and copies ran while one was open for 24% -> 22% of each run, Pallas kernels for 20% -> 18%
where the time goes in v4:
time: 214 us; the launch traced here: 213 us
  waiting for transfers between devices  57.2 us (27%)
  starting transfers between devices  42.4 us (20%)
  Pallas kernels  38.4 us (18%)
  local copies, waits for them, and re-layouts  26 us (12%)
  other arithmetic  24.2 us (11%)
  between operations  14.6 us (7%)
  matrix products  10.1 us (5%)
    ppermute x13, waiting for transfers between devices, fetch(): return lax.ppermute(v, axis, [((i + step) % n, i) for i in range(n)])  29.2 us
    pallas_call x1, Pallas kernels, backward(): pl.pallas_call(backward_kernel, out_shape=jax.ShapeDtypeStruct((tokens, w...  22.8 us
    pallas_call x1, Pallas kernels, forward(): pl.pallas_call(forward_kernel, out_shape=jax.ShapeDtypeStruct((tokens, co...  15.6 us
    ppermute x13, starting transfers between devices, fetch(): return lax.ppermute(v, axis, [((i + step) % n, i) for i in range(n)])  14.8 us
    all_to_all x1, waiting for transfers between devices, body(): g_got = lax.all_to_all(g_send, DP, 0, 0, tiled=True)  14.1 us
    all_to_all x1, waiting for transfers between devices, body(): narrow = lax.all_to_all(narrow, DP, 0, 0, tiled=True)  11 us
    dot_general x4, matrix products, dot(): return lax.dot_general(a, b, (dims, ((), ())), preferred_element_type=F32)  10.1 us
    all_to_all x1, starting transfers between devices, body(): flags = lax.all_to_all(sent, DP, 0, 0, tiled=True)  8.6 us
  transfers between devices with their start and end apart: 19, of which 12 were waited for; matrix products, arithmetic and copies ran while one was open for 22% of the time, Pallas kernels for 18%

profile of v4, /device:TPU:1, one launch (start us, length us, event | category | flops | bytes accessed | tf_op | source)
XLA Modules:
  0.0 212.9 jit_solution(11750089728805246967)
XLA Ops:
  7.3 3.4 %fusion = f32[512]{0:T(512)S(1)} fusion(bf16[512,4608]{1,0:T(8,128)(2,1)} %x.1), kind=kLoop, calls=%fused_computation.9 | loop fusion | flops 7077376 | bytes 4720640 | tf_op jit(solution)/shard_map/reduce_sum | solution.py:199
  12.3 4.7 %collective-permute-start = (bf16[1152,128]{1,0:T(8,128)(2,1)S(1)}, bf16[1152,128]{1,0:T(8,128)(2,1)}, u32[]{:S(2)}, u32[]{:S(2)}) collective-permute-start(bf16[1152,128]{1,0:T(8,128)(2,1)S(1)} %copy-done.8), channel_id=1, source_target_pairs={{1,0},{2,1},{3,2},{0,3},{5,4},{6,5},{7,6},{4,7},{9,8},{10,9},{11,1... | collective-permute-start | bytes 884744 | tf_op jit(solution)/shard_map/ppermute | solution.py:20
  18.6 8.6 %all-to-all-start = ((s32[32,1,1]{2,1,0:T(1,128)}), s32[32,1,1]{2,1,0:T(1,128)S(1)}, u32[]{:S(2)}, u32[]{:S(2)}) async-start(s32[32,1,1]{2,1,0:T(1,128)} %copy.29), calls=%async_computation | async-start | bytes 32768 | tf_op jit(solution)/shard_map/all_to_all | solution.py:190
  29.5 6.1 %fusion.2.xn = bf16[512,4608]{1,0:T(8,128)(2,1)} fusion(bf16[512,4608]{1,0:T(8,128)(2,1)} %x.1, f32[4608]{0:T(1024)S(1)} %convert_element_type.58, f32[512]{0:T(512)S(1)} %add_rsqrt_fusion), kind=kLoop, calls=%fused_computation.11 | loop fusion | flops 9437184 | bytes 9457664 | tf_op jit(solution)/shard_map/convert_element_type | solution.py:204
  40.2 3.7 %convolution_convert_fusion.low = bf16[512,128]{1,0:T(8,128)(2,1)S(1)} fusion(bf16[512,4608]{1,0:T(8,128)(2,1)} %fusion.2.xn, bf16[4608,128]{1,0:T(8,128)(2,1)S(1)} %constant_dynamic-update-slice_fusion.down), kind=kOutput, calls=%fused_computation.22 | convolution fusion | flops 604045312 | bytes 6029312 | tf_op jit(solution)/shard_map/dot_general | solution.py:15
  45.4 7.4 %all-to-all-start.1 = ((bf16[32,16,256]{2,1,0:T(8,128)(2,1)}), bf16[32,16,256]{2,1,0:T(8,128)(2,1)S(1)}, u32[]{:S(2)}, u32[]{:S(2)}) async-start(bf16[32,16,256]{2,1,0:T(8,128)(2,1)} %pad_maximum_fusion), calls=%async_computation.1 | async-start | bytes 524288 | tf_op jit(solution)/shard_map/all_to_all | solution.py:216
  52.8 11.0 %all-to-all-done.1 = bf16[32,16,256]{2,1,0:T(8,128)(2,1)S(1)} async-done(((bf16[32,16,256]{2,1,0:T(8,128)(2,1)}), bf16[32,16,256]{2,1,0:T(8,128)(2,1)S(1)}, u32[]{:S(2)}, u32[]{:S(2)}) %all-to-all-start.1) | async-done | bytes 262176 | tf_op jit(solution)/shard_map/all_to_all | solution.py:216
  67.0 4.1 %fusion.14 = f32[4608,128]{1,0:T(8,128)S(1)} fusion(bf16[512,4608]{1,0:T(8,128)(2,1)} %fusion.2.xn, bf16[512,128]{1,0:T(8,128)(2,1)S(1)} %bitcast.53), kind=kOutput, calls=%fused_computation.79 | convolution fusion | flops 603979776 | bytes 7208960 | tf_op jit(solution)/shard_map/dot_general | solution.py:15
  75.5 3.2 %broadcast_select_fusion = bf16[32,16,2048]{2,1,0:T(8,128)(2,1)} fusion(bf16[32,16,2048]{2,1,0:T(8,128)(2,1)} %gather_fusion.2, pred[32]{0:T(512)(128)(4,1)S(1)} %compare_and_fusion.2), kind=kLoop, calls=%fused_computation.18 | loop fusion | flops 1048576 | bytes 4194336 | tf_op jit(solution)/shard_map/jit(_take)/select_n | solution.py:221
  78.7 4.7 %all-to-all-start.2 = ((bf16[32,16,2048]{2,1,0:T(8,128)(2,1)}), bf16[32,16,2048]{2,1,0:T(8,128)(2,1)}, u32[]{:S(2)}, u32[]{:S(2)}) async-start(bf16[32,16,2048]{2,1,0:T(8,128)(2,1)} %broadcast_select_fusion), calls=%async_computation.2 | async-start | bytes 4194304 | tf_op jit(solution)/shard_map/all_to_all | solution.py:223
  83.7 2.3 %fusion.6 = f32[3328,128]{1,0:T(8,128)S(1)} fusion(f32[3328,128]{1,0:T(8,128)} %collective-permute-done.3, s32[]{:T(128)S(6)} %select_n.236, f32[4608,128]{1,0:T(8,128)} %copy-done.2, f32[2048,128]{1,0:T(8,128)S(1)} %bitcast.59), kind=kLoop, calls=%fused_computation.21 | loop fusion | flops 851968 | bytes 6815748 | tf_op jit(solution)/shard_map/add | solution.py:49
  90.7 8.3 %collective-permute-done.4 = bf16[832,128]{1,0:T(8,128)(2,1)S(1)} collective-permute-done((bf16[832,128]{1,0:T(8,128)(2,1)S(1)}, bf16[832,128]{1,0:T(8,128)(2,1)S(1)}, u32[]{:S(2)}, u32[]{:S(2)}) %collective-permute-start.4) | collective-permute-done | bytes 213024 | tf_op jit(solution)/shard_map/ppermute | solution.py:20
  99.0 2.7 %collective-permute-done.5 = bf16[832,128]{1,0:T(8,128)(2,1)S(1)} collective-permute-done((bf16[832,128]{1,0:T(8,128)(2,1)S(1)}, bf16[832,128]{1,0:T(8,128)(2,1)S(1)}, u32[]{:S(2)}, u32[]{:S(2)}) %collective-permute-start.5) | collective-permute-done | bytes 213024 | tf_op jit(solution)/shard_map/ppermute | solution.py:20
  101.7 5.8 %collective-permute-done.6 = bf16[832,128]{1,0:T(8,128)(2,1)S(1)} collective-permute-done((bf16[832,128]{1,0:T(8,128)(2,1)S(1)}, bf16[832,128]{1,0:T(8,128)(2,1)S(1)}, u32[]{:S(2)}, u32[]{:S(2)}) %collective-permute-start.6) | collective-permute-done | bytes 213024 | tf_op jit(solution)/shard_map/ppermute | solution.py:20
  108.6 14.1 %all-to-all-done.2 = bf16[32,16,2048]{2,1,0:T(8,128)(2,1)} async-done(((bf16[32,16,2048]{2,1,0:T(8,128)(2,1)}), bf16[32,16,2048]{2,1,0:T(8,128)(2,1)}, u32[]{:S(2)}, u32[]{:S(2)}) %all-to-all-start.2) | async-done | bytes 2097184 | tf_op jit(solution)/shard_map/all_to_all | solution.py:223
  128.6 3.1 %collective-permute-done.9 = f32[208,128]{1,0:T(8,128)S(1)} collective-permute-done((f32[208,128]{1,0:T(8,128)S(1)}, f32[208,128]{1,0:T(8,128)S(1)}, u32[]{:S(2)}, u32[]{:S(2)}) %collective-permute-start.9) | collective-permute-done | bytes 106528 | tf_op jit(solution)/shard_map/ppermute | solution.py:20
  131.7 2.6 %collective-permute-start.10 = (f32[208,128]{1,0:T(8,128)S(1)}, f32[208,128]{1,0:T(8,128)S(1)}, u32[]{:S(2)}, u32[]{:S(2)}) collective-permute-start(f32[208,128]{1,0:T(8,128)S(1)} %get-tuple-element.18), channel_id=1, source_target_pairs={{8,0},{16,8},{24,16},{0,24},{9,1},{17,9},{25,17},{1,25},{10,2},{18... | collective-permute-start | bytes 319496 | tf_op jit(solution)/shard_map/ppermute | solution.py:20
  136.7 2.8 %collective-permute-done.11 = f32[208,128]{1,0:T(8,128)S(1)} collective-permute-done((f32[208,128]{1,0:T(8,128)S(1)}, f32[208,128]{1,0:T(8,128)S(1)}, u32[]{:S(2)}, u32[]{:S(2)}) %collective-permute-start.11) | collective-permute-done | bytes 106528 | tf_op jit(solution)/shard_map/ppermute | solution.py:20
  141.7 2.3 %copy-done = bf16[512,4608]{1,0:T(8,128)(2,1)S(1)} copy-done((bf16[512,4608]{1,0:T(8,128)(2,1)S(1)}, bf16[512,4608]{1,0:T(8,128)(2,1)}, u32[]{:S(2)}) %copy-start) | copy-done | bytes 4718616
  144.0 15.6 %forward.1 = bf16[512,2048]{1,0:T(8,128)(2,1)} custom-call(s32[32]{0:T(128)S(1)} %select_reduce_fusion.source, bf16[512,4608]{1,0:T(8,128)(2,1)S(1)} %copy-done, bf16[512,128]{1,0:T(8,128)(2,1)S(1)} %convolution_convert_fusion.low, bf16[2,4608,1024]{2,1,0:T(8,128)(2,1)} %bitcast.67, bf16[128,2048]{1,0:T(8,128)(2,1)S(1)} %copy-done.1), custom_call_target="tpu_custom_call" | custom-call | flops 9663676416 | bytes 27262976 | tf_op jit(solution)/shard_map/forward/pallas_call | solution.py:83
  159.6 6.6 %all-to-all-start.3 = ((bf16[32,16,2048]{2,1,0:T(8,128)(2,1)}), bf16[32,16,2048]{2,1,0:T(8,128)(2,1)}, u32[]{:S(2)}, u32[]{:S(2)}) async-start(bf16[32,16,2048]{2,1,0:T(8,128)(2,1)} %bitcast.21), calls=%async_computation.3 | async-start | bytes 4194304 | tf_op jit(solution)/shard_map/all_to_all | solution.py:243
  166.9 3.6 %gather_fusion.4 = bf16[32,16,2048]{2,1,0:T(8,128)(2,1)} fusion(bf16[32,16,2048]{2,1,0:T(8,128)(2,1)} %all-to-all-done.2, s32[1024]{0:T(1024)S(1)} %pad_clamp_fusion.1), kind=kCustom, calls=%fused_computation.6 | custom fusion | bytes 4194432 | tf_op jit(solution)/shard_map/jit(_take)/gather | solution.py:224
  172.5 22.8 %backward.1 = bf16[512,4608]{1,0:T(8,128)(2,1)} custom-call(s32[32]{0:T(128)S(1)} %get-tuple-element.29.live, bf16[512,2048]{1,0:T(8,128)(2,1)S(1)} %fusion.3.g, bf16[512,128]{1,0:T(8,128)(2,1)S(1)} %bitcast.54, bf16[2,4608,1024]{2,1,0:T(8,128)(2,1)} %bitcast.68, bf16[4608,128]{1,0:T(8,128)(2,1)S(1)} %constant_dynamic-update-slice_fusion.down, ...), custom_call_target="tpu_custom_call" | custom-call | flops 9663676416 | bytes 33554432 | tf_op jit(solution)/shard_map/backward/pallas_call | solution.py:147
  195.2 2.8 %all-to-all-done.3 = bf16[32,16,2048]{2,1,0:T(8,128)(2,1)} async-done(((bf16[32,16,2048]{2,1,0:T(8,128)(2,1)}), bf16[32,16,2048]{2,1,0:T(8,128)(2,1)}, u32[]{:S(2)}, u32[]{:S(2)}) %all-to-all-start.3) | async-done | bytes 2097184 | tf_op jit(solution)/shard_map/all_to_all | solution.py:243
  (116 shorter events, 45.8 us)
Async XLA Ops:
  7.2 134.5 %all-gather.3.cloned.1.call-start = ((), (), s32[]{:S(2)}) async-start(), calls=%async_computation.4 | async-start | bytes 19021824 | tf_op jit(solution)/shard_map/all_gather | solution.py:38
  7.2 10.5 %copy-start.11 = (s32[32]{0:T(128)S(1)}, s32[32]{0:T(128)}, u32[]{:S(2)}) copy-start(s32[32]{0:T(128)} %param.16) | copy-start | bytes 388
  7.2 10.5 %copy-start.10 = (s32[32]{0:T(128)S(1)}, s32[32]{0:T(128)}, u32[]{:S(2)}) copy-start(s32[32]{0:T(128)} %param.15) | copy-start | bytes 388
  7.2 20.0 %copy-start.9 = (bf16[4608]{0:T(1024)(128)(2,1)S(1)}, bf16[4608]{0:T(1024)(128)(2,1)}, u32[]{:S(2)}) copy-start(bf16[4608]{0:T(1024)(128)(2,1)} %param.11) | copy-start | bytes 27652
  7.3 20.0 %copy-start.3 = (bf16[256,2048]{1,0:T(8,128)(2,1)S(1)}, bf16[256,2048]{1,0:T(8,128)(2,1)}, u32[]{:S(2)}) copy-start(bf16[256,2048]{1,0:T(8,128)(2,1)} %param.17) | copy-start | bytes 3145732
  12.3 16.6 %copy-start.1 = (bf16[128,2048]{1,0:T(8,128)(2,1)S(1)}, bf16[128,2048]{1,0:T(8,128)(2,1)}, u32[]{:S(2)}) copy-start(bf16[128,2048]{1,0:T(8,128)(2,1)} %up.1) | copy-start | bytes 1572868
  12.3 24.8 %collective-permute-start = (bf16[1152,128]{1,0:T(8,128)(2,1)S(1)}, bf16[1152,128]{1,0:T(8,128)(2,1)}, u32[]{:S(2)}, u32[]{:S(2)}) collective-permute-start(bf16[1152,128]{1,0:T(8,128)(2,1)S(1)} %copy-done.8), channel_id=1, source_target_pairs={{1,0},{2,1},{3,2},{0,3},{5,4},{6,5},{7,6},{4,7},{9,8},{10,9},{11,1... | collective-permute-start | bytes 884744 | tf_op jit(solution)/shard_map/ppermute | solution.py:20
  17.0 21.1 %collective-permute-start.1 = (bf16[1152,128]{1,0:T(8,128)(2,1)S(1)}, bf16[1152,128]{1,0:T(8,128)(2,1)}, u32[]{:S(2)}, u32[]{:S(2)}) collective-permute-start(bf16[1152,128]{1,0:T(8,128)(2,1)S(1)} %copy-done.8), channel_id=1, source_target_pairs={{2,0},{3,1},{0,2},{1,3},{6,4},{7,5},{4,6},{5,7},{10,8},{11,9},{8,1... | collective-permute-start | bytes 884744 | tf_op jit(solution)/shard_map/ppermute | solution.py:20
  17.0 22.2 %collective-permute-start.2 = (bf16[1152,128]{1,0:T(8,128)(2,1)S(1)}, bf16[1152,128]{1,0:T(8,128)(2,1)}, u32[]{:S(2)}, u32[]{:S(2)}) collective-permute-start(bf16[1152,128]{1,0:T(8,128)(2,1)S(1)} %copy-done.8), channel_id=1, source_target_pairs={{3,0},{0,1},{1,2},{2,3},{7,4},{4,5},{5,6},{6,7},{11,8},{8,9},{9,10... | collective-permute-start | bytes 884744 | tf_op jit(solution)/shard_map/ppermute | solution.py:20
  18.6 17.0 %all-to-all-start = ((s32[32,1,1]{2,1,0:T(1,128)}), s32[32,1,1]{2,1,0:T(1,128)S(1)}, u32[]{:S(2)}, u32[]{:S(2)}) async-start(s32[32,1,1]{2,1,0:T(1,128)} %copy.29), calls=%async_computation | async-start | bytes 32768 | tf_op jit(solution)/shard_map/all_to_all | solution.py:190
  45.4 18.4 %all-to-all-start.1 = ((bf16[32,16,256]{2,1,0:T(8,128)(2,1)}), bf16[32,16,256]{2,1,0:T(8,128)(2,1)S(1)}, u32[]{:S(2)}, u32[]{:S(2)}) async-start(bf16[32,16,256]{2,1,0:T(8,128)(2,1)} %pad_maximum_fusion), calls=%async_computation.1 | async-start | bytes 524288 | tf_op jit(solution)/shard_map/all_to_all | solution.py:216
  73.2 10.5 %collective-permute-start.3 = (f32[3328,128]{1,0:T(8,128)}, f32[3328,128]{1,0:T(8,128)}, u32[]{:S(2)}, u32[]{:S(2)}) collective-permute-start(f32[3328,128]{1,0:T(8,128)} %fusion.4), channel_id=1, source_target_pairs={{4,0},{0,4},{5,1},{1,5},{6,2},{2,6},{7,3},{3,7},{12,8},{8,12},{13,... | collective-permute-start | bytes 5111816 | tf_op jit(solution)/shard_map/ppermute | solution.py:20
  78.7 44.1 %all-to-all-start.2 = ((bf16[32,16,2048]{2,1,0:T(8,128)(2,1)}), bf16[32,16,2048]{2,1,0:T(8,128)(2,1)}, u32[]{:S(2)}, u32[]{:S(2)}) async-start(bf16[32,16,2048]{2,1,0:T(8,128)(2,1)} %broadcast_select_fusion), calls=%async_computation.2 | async-start | bytes 4194304 | tf_op jit(solution)/shard_map/all_to_all | solution.py:223
  83.4 118.1 %all-gather.5.cloned.1.call-start = ((), (), s32[]{:S(2)}) async-start(), calls=%async_computation.5 | async-start | bytes 1757184 | tf_op jit(solution)/shard_map/all_gather | solution.py:237
  87.2 11.8 %collective-permute-start.4 = (bf16[832,128]{1,0:T(8,128)(2,1)S(1)}, bf16[832,128]{1,0:T(8,128)(2,1)S(1)}, u32[]{:S(2)}, u32[]{:S(2)}) collective-permute-start(bf16[832,128]{1,0:T(8,128)(2,1)S(1)} %get-tuple-element.21), channel_id=1, source_target_pairs={{1,0},{2,1},{3,2},{0,3},{5,4},{6,5},{7,6},{4,7},{9,8},{10,9},{11,1... | collective-permute-start | bytes 638984 | tf_op jit(solution)/shard_map/ppermute | solution.py:20
  88.8 13.0 %collective-permute-start.5 = (bf16[832,128]{1,0:T(8,128)(2,1)S(1)}, bf16[832,128]{1,0:T(8,128)(2,1)S(1)}, u32[]{:S(2)}, u32[]{:S(2)}) collective-permute-start(bf16[832,128]{1,0:T(8,128)(2,1)S(1)} %get-tuple-element.23), channel_id=1, source_target_pairs={{2,0},{3,1},{0,2},{1,3},{6,4},{7,5},{4,6},{5,7},{10,8},{11,9},{8,1... | collective-permute-start | bytes 638984 | tf_op jit(solution)/shard_map/ppermute | solution.py:20
  90.7 16.8 %collective-permute-start.6 = (bf16[832,128]{1,0:T(8,128)(2,1)S(1)}, bf16[832,128]{1,0:T(8,128)(2,1)S(1)}, u32[]{:S(2)}, u32[]{:S(2)}) collective-permute-start(bf16[832,128]{1,0:T(8,128)(2,1)S(1)} %get-tuple-element.22), channel_id=1, source_target_pairs={{3,0},{0,1},{1,2},{2,3},{7,4},{4,5},{5,6},{6,7},{11,8},{8,9},{9,10... | collective-permute-start | bytes 638984 | tf_op jit(solution)/shard_map/ppermute | solution.py:20
  122.8 3.6 %collective-permute-start.7 = (f32[208,128]{1,0:T(8,128)S(1)}, f32[208,128]{1,0:T(8,128)S(1)}, u32[]{:S(2)}, u32[]{:S(2)}) collective-permute-start(f32[208,128]{1,0:T(8,128)S(1)} %get-tuple-element.24), channel_id=1, source_target_pairs={{32,0},{64,32},{96,64},{0,96},{33,1},{65,33},{97,65},{1,97},{34,2}... | collective-permute-start | bytes 319496 | tf_op jit(solution)/shard_map/ppermute | solution.py:20
  123.5 5.1 %collective-permute-start.8 = (f32[208,128]{1,0:T(8,128)S(1)}, f32[208,128]{1,0:T(8,128)S(1)}, u32[]{:S(2)}, u32[]{:S(2)}) collective-permute-start(f32[208,128]{1,0:T(8,128)S(1)} %get-tuple-element.26), channel_id=1, source_target_pairs={{64,0},{96,32},{0,64},{32,96},{65,1},{97,33},{1,65},{33,97},{66,2}... | collective-permute-start | bytes 319496 | tf_op jit(solution)/shard_map/ppermute | solution.py:20
  124.4 7.3 %collective-permute-start.9 = (f32[208,128]{1,0:T(8,128)S(1)}, f32[208,128]{1,0:T(8,128)S(1)}, u32[]{:S(2)}, u32[]{:S(2)}) collective-permute-start(f32[208,128]{1,0:T(8,128)S(1)} %get-tuple-element.25), channel_id=1, source_target_pairs={{96,0},{0,32},{32,64},{64,96},{97,1},{1,33},{33,65},{65,97},{98,2}... | collective-permute-start | bytes 319496 | tf_op jit(solution)/shard_map/ppermute | solution.py:20
  131.7 4.9 %collective-permute-start.10 = (f32[208,128]{1,0:T(8,128)S(1)}, f32[208,128]{1,0:T(8,128)S(1)}, u32[]{:S(2)}, u32[]{:S(2)}) collective-permute-start(f32[208,128]{1,0:T(8,128)S(1)} %get-tuple-element.18), channel_id=1, source_target_pairs={{8,0},{16,8},{24,16},{0,24},{9,1},{17,9},{25,17},{1,25},{10,2},{18... | collective-permute-start | bytes 319496 | tf_op jit(solution)/shard_map/ppermute | solution.py:20
  134.4 5.2 %collective-permute-start.11 = (f32[208,128]{1,0:T(8,128)S(1)}, f32[208,128]{1,0:T(8,128)S(1)}, u32[]{:S(2)}, u32[]{:S(2)}) collective-permute-start(f32[208,128]{1,0:T(8,128)S(1)} %get-tuple-element.18), channel_id=1, source_target_pairs={{16,0},{24,8},{0,16},{8,24},{17,1},{25,9},{1,17},{9,25},{18,2},{26... | collective-permute-start | bytes 319496 | tf_op jit(solution)/shard_map/ppermute | solution.py:20
  134.4 6.6 %collective-permute-start.12 = (f32[208,128]{1,0:T(8,128)S(1)}, f32[208,128]{1,0:T(8,128)S(1)}, u32[]{:S(2)}, u32[]{:S(2)}) collective-permute-start(f32[208,128]{1,0:T(8,128)S(1)} %get-tuple-element.18), channel_id=1, source_target_pairs={{24,0},{0,8},{8,16},{16,24},{25,1},{1,9},{9,17},{17,25},{26,2},{2,... | collective-permute-start | bytes 319496 | tf_op jit(solution)/shard_map/ppermute | solution.py:20
  159.6 38.5 %all-to-all-start.3 = ((bf16[32,16,2048]{2,1,0:T(8,128)(2,1)}), bf16[32,16,2048]{2,1,0:T(8,128)(2,1)}, u32[]{:S(2)}, u32[]{:S(2)}) async-start(bf16[32,16,2048]{2,1,0:T(8,128)(2,1)} %bitcast.21), calls=%async_computation.3 | async-start | bytes 4194304 | tf_op jit(solution)/shard_map/all_to_all | solution.py:243
  (7 other events, 21.8 us)
Sparse Core Ops, SparseCore 0:
  12.4 109.1 all-gather.2
  141.8 46.9 all-gather.4
